TPU v7x, 32 devices: a whole 2x2x4 slice. The times are simulated.
32 devices in a mesh: ctx: 4 (over y, core), pb: 8 (over z, x).
Axes of the slice: x: 2, y: 2, z: 4, core: 2. Of those that a mesh axis runs over, the one named last changes fastest.
Arguments:
- queries: bfloat16 [128, 64, 8, 128], P('pb'), may hold values from -6 to 6
- keys: bfloat16 [4096, 128], P('ctx'), may hold values from -6 to 6
- values: bfloat16 [4096, 128], P('ctx'), may hold values from -6 to 6
- outputs_saved: bfloat16 [128, 64, 8, 128], P('pb'), may hold values from -6 to 6
- grad_out: bfloat16 [128, 64, 8, 128], P('pb'), may hold values from -6 to 6
- saved_lse: float32 [128, 64, 8], P('pb'), may hold values from 7 to 9
- block_lists: int32 [128, 24], P('pb'), may hold values from -1 to 31, as said below
Outputs:
- query_grad: float32 [128, 64, 8, 128], P('pb', 'ctx')
- key_grad: float32 [4096, 128], P(('ctx', 'pb'))
- value_grad: float32 [4096, 128], P(('ctx', 'pb'))
Inputs may be any that keep to these rules, and one draw needn't show every extreme that they name: `block_lists`: each row lists distinct blocks in rising order, then -1 in the remaining entries. Of one row's blocks at most 6 lie in one run of 8 blocks (j * 8 to j * 8 + 7), and in every row exactly 6 lie in some such run.
All inputs are finite; a program needn't handle non-finite values.
Results may differ from a plain program's by a relative error of at most 0.0029.
Values sent between devices are 32-bit elements; how exact they have to be, the bound alone decides.
No kernel may reach another device: no remote copies, remote signals or barrier semaphores. Data moves between devices by JAX's collectives and lax.ppermute only.
A program may use at most 128 MiB of HBM per device.

v0:
```python
from functools import partial

import jax
import jax.numpy as jnp
from jax import lax
from jax.sharding import PartitionSpec as P

BLK = 128
CAP = 6
BLK_DEV = 8


def slot_table(block_lists, local_blocks, shard_index, slot_count):
    first_block = shard_index * local_blocks
    offset = block_lists - first_block
    inside = (block_lists >= 0) & (offset >= 0) & (offset < local_blocks)
    blocks = jnp.arange(local_blocks, dtype=jnp.int32)
    member = jnp.any(inside[:, :, None] & (offset[:, :, None] == blocks[None, None, :]), axis=1)
    position = jnp.cumsum(member.astype(jnp.int32), axis=1) - 1
    wanted = jnp.arange(slot_count, dtype=jnp.int32)
    slot_hit = member[:, None, :] & (position[:, None, :] == wanted[None, :, None])
    chosen = jnp.sum(slot_hit.astype(jnp.int32) * blocks[None, None, :], axis=2)
    live_slots = jnp.any(slot_hit, axis=2)
    return (chosen, live_slots)


def tile_terms(q_rows, dout_rows, lse_rows, delta_rows, key_slab, value_slab, live_cols, factor):
    scores = factor * jnp.einsum("rd,kd->rk", q_rows, key_slab, preferred_element_type=jnp.float32)
    prob_tile = jnp.where(live_cols[None, :], jnp.exp(scores - lse_rows[:, None]), 0.0)
    dprob_tile = jnp.einsum("rd,kd->rk", dout_rows, value_slab, preferred_element_type=jnp.float32)
    dscore = (prob_tile * (dprob_tile - delta_rows[:, None])).astype(jnp.bfloat16)
    return (prob_tile, dscore)


def question_step(keep_rows, factor, carry, element):
    q_all, dout_all, lse_all, delta_all, slab_k, slab_v, cols = element
    head_width = q_all.shape[-1]
    q_rows = q_all.reshape(-1, head_width)
    dout_rows = dout_all.reshape(-1, head_width)
    prob_tile, dscore = tile_terms(
        q_rows, dout_rows, lse_all.reshape(-1), delta_all.reshape(-1), slab_k, slab_v, cols, factor
    )
    key_part = factor * jnp.einsum("rk,rd->kd", dscore, q_rows, preferred_element_type=jnp.float32)
    value_part = jnp.einsum(
        "rk,rd->kd", prob_tile.astype(jnp.bfloat16), dout_rows, preferred_element_type=jnp.float32
    )
    query_part = factor * jnp.dot(dscore, slab_k, preferred_element_type=jnp.float32)
    return (carry, (key_part, value_part, query_part.reshape(q_all.shape)))


def local(queries, keys, values, outputs_saved, grad_out, saved_lse, block_lists):
    head_width = queries.shape[-1]
    factor = head_width ** (-0.5)
    local_blocks = BLK_DEV
    block_rows = BLK
    slot_count = CAP
    key_blocks = keys.reshape(local_blocks, block_rows, head_width)
    value_blocks = values.reshape(local_blocks, block_rows, head_width)
    shard_index = lax.axis_index("ctx")
    chosen, live_slots = slot_table(block_lists, local_blocks, shard_index, slot_count)
    question_count = chosen.shape[0]
    key_slab = key_blocks[chosen].reshape(question_count, slot_count * block_rows, head_width)
    value_slab = value_blocks[chosen].reshape(question_count, slot_count * block_rows, head_width)
    live_cols = jnp.repeat(live_slots, block_rows, axis=1)
    row_delta = jnp.sum(grad_out.astype(jnp.float32) * outputs_saved.astype(jnp.float32), axis=-1)
    scanned = (queries, grad_out, saved_lse, row_delta, key_slab, value_slab, live_cols)
    stepper = partial(question_step, True, factor)
    unused_carry, (key_parts, value_parts, query_part) = lax.scan(stepper, 0, scanned)
    flat_chosen = chosen.reshape(-1)
    zero_acc = jnp.zeros((local_blocks, block_rows, head_width), jnp.float32)
    key_acc = zero_acc.at[flat_chosen].add(key_parts.reshape(-1, block_rows, head_width))
    value_acc = zero_acc.at[flat_chosen].add(value_parts.reshape(-1, block_rows, head_width))
    key_grad, value_grad = (
        lax.psum_scatter(key_acc.reshape(-1, head_width), "pb", scatter_dimension=0, tiled=True),
        lax.psum_scatter(value_acc.reshape(-1, head_width), "pb", scatter_dimension=0, tiled=True),
    )
    query_grad = lax.psum_scatter(query_part, "ctx", scatter_dimension=1, tiled=True)
    return (query_grad, key_grad, value_grad)


def solution(mesh):
    placed = (
        P("pb", None, None, None),
        P("ctx", None),
        P("ctx", None),
        P("pb", None, None, None),
        P("pb", None, None, None),
        P("pb", None, None),
        P("pb", None),
    )
    return jax.shard_map(
        local,
        mesh=mesh,
        in_specs=placed,
        out_specs=(P("pb", "ctx", None, None), P(("ctx", "pb"), None), P(("ctx", "pb"), None)),
        check_vma=False,
    )
```

profile of v0, /device:TPU:0, one launch (start us, length us, event | category | flops | bytes accessed | tf_op | source)
XLA Modules:
  0.0 369.5 jit_solution(16004083109603989497)
XLA Ops:
  9.7 2.8 gather_fusion.1
  12.4 2.7 gather_fusion
  15.4 2.8 multiply_reduce_fusion
  18.1 159.9 %while.14 = (s32[]{:T(128)}, f32[16,768,128]{2,1,0:T(8,128)}, f32[16,768,128]{2,1,0:T(8,128)}, f32[16,64,8,128]{3,2,0,1:T(8,128)}, pred[16,768]{1,0:T(8,128)(4,1...) while((s32[]{:T(128)}, f32[16,768,128]{2,1,0:T(8,128)}, ...), condition=%wide.region_6.7_spmd, body=%wide.region_5.6_spmd.sunk | while | flops 506232832 | bytes 9272705 | solution.py:68
  24.0 2.1 fusion.56
  32.0 2.1 fusion.55
  34.0 2.1 fusion.56
  42.0 2.1 fusion.55
  44.0 2.1 fusion.56
  51.9 2.1 fusion.55
  71.9 2.1 fusion.55
  74.0 2.1 fusion.56
  82.0 2.1 fusion.55
  84.0 2.1 fusion.56
  92.0 2.1 fusion.55
  94.0 2.1 fusion.56
  102.0 2.1 fusion.55
  114.0 2.1 fusion.56
  131.9 2.1 fusion.55
  134.0 2.1 fusion.56
  141.9 2.1 fusion.55
  144.0 2.1 fusion.56
  152.0 2.1 fusion.55
  161.9 2.1 fusion.55
  171.9 2.1 fusion.55
  174.0 2.1 fusion.56
  178.1 6.5 %copy.35 = f32[8,8,128,128]{3,1,2,0:T(8,128)} copy(f32[8,8,128,128]{3,2,1,0:T(8,128)} %bitcast.27) | data formatting | bytes 8388608
  184.9 13.2 %scatter_fusion = f32[8,128,128]{2,1,0:T(8,128)S(1)} fusion(f32[8,128,128]{2,1,0:T(8,128)S(1)} %broadcast_in_dim.48.clone, s32[96]{0:T(128)S(1)} %fusion.29, f32[96,128,128]{2,1,0:T(8,128)} %bitcast.94), kind=kCustom, calls=%fused_computation.2 | custom fusion | flops 1572864 | bytes 18874752 | tf_op jit(solution)/shard_map/scatter-add | solution.py:71
  199.0 13.2 %scatter_fusion.1 = f32[8,128,128]{2,1,0:T(8,128)S(1)} fusion(f32[8,128,128]{2,1,0:T(8,128)S(1)} %broadcast_in_dim.48.clone.1, s32[96]{0:T(128)S(1)} %fusion.29, f32[96,128,128]{2,1,0:T(8,128)} %bitcast.95), kind=kCustom, calls=%fused_computation.3 | custom fusion | flops 1572864 | bytes 18874752 | tf_op jit(solution)/shard_map/scatter-add | solution.py:72
  213.0 19.0 %reduce-scatter.11.cloned.1.call-done = f32[16,16384]{1,0:T(8,128)} async-done(((f32[64,16384]{1,0:T(8,128)}), f32[16,16384]{1,0:T(8,128)}) %reduce-scatter.11.cloned.1.call-update) | async-done | bytes 1048592
  234.5 63.7 %reduce-scatter.7.cloned.1.call-done = f32[128,128]{1,0:T(8,128)} async-done(((f32[1024,128]{1,0:T(8,128)}), f32[128,128]{1,0:T(8,128)}) %reduce-scatter.7.cloned.1.call-update) | async-done | bytes 65552 | tf_op jit(solution)/shard_map/reduce_scatter | solution.py:74
  298.1 64.9 %reduce-scatter.9.cloned.1.call-done = f32[128,128]{1,0:T(8,128)} async-done(((f32[1024,128]{1,0:T(8,128)}), f32[128,128]{1,0:T(8,128)}) %reduce-scatter.9.cloned.1.call-update) | async-done | bytes 65552 | tf_op jit(solution)/shard_map/reduce_scatter | solution.py:75
  (197 shorter events, 120.9 us)
Async XLA Ops:
  7.2 2.5 copy-start
  7.2 224.8 %reduce-scatter.11.cloned.1.call-start = ((), (), s32[]{:S(2)}) async-start(), calls=%async_computation.5 | async-start | bytes 5242880
  9.6 2.8 copy-start.3
  12.4 2.9 copy-start.4
  184.6 113.6 %reduce-scatter.7.cloned.1.call-start = ((), (), s32[]{:S(2)}) async-start(), calls=%async_computation.3 | async-start | bytes 589824 | tf_op jit(solution)/shard_map/reduce_scatter | solution.py:74
  198.1 0.8 copy-start.2
  198.9 164.1 %reduce-scatter.9.cloned.1.call-start = ((), (), s32[]{:S(2)}) async-start(), calls=%async_computation.4 | async-start | bytes 589824 | tf_op jit(solution)/shard_map/reduce_scatter | solution.py:75
  212.2 0.8 copy-start.1
Sparse Core Ops, SparseCore 0:
  184.7 47.2 reduce-scatter.10
  236.2 61.8 reduce-scatter.6
  302.1 60.9 reduce-scatter.8
where the time goes:
time: 372 us; the launch traced here: 370 us
  waiting for transfers between devices  148 us (40%)
  matrix products  144 us (39%)
  local copies, waits for them, and re-layouts  32.7 us (9%)
  other arithmetic  31.2 us (8%)
  between operations  13.9 us (4%)
    reduce_scatter x1, waiting for transfers between devices, local(): lax.psum_scatter(value_acc.reshape(-1, head_width), 'pb', scatter_dimensi...  64.9 us
    reduce_scatter x1, waiting for transfers between devices, local(): lax.psum_scatter(key_acc.reshape(-1, head_width), 'pb', scatter_dimension...  63.7 us
    dot_general x16, matrix products, question_step(): jnp.einsum('rk,rd->kd', prob_tile.astype(jnp.bfloat16), dout_rows, prefer...  33.1 us
    dot_general x16, matrix products, question_step(): jnp.einsum('rk,rd->kd', dscore, q_rows, preferred_element_type=jnp.float32)  33.1 us
    dot_general x16, matrix products, question_step(): jnp.dot(dscore, slab_k, preferred_element_type=jnp.float32)  32.4 us
    dot_general x16, matrix products, tile_terms(): jnp.einsum('rd,kd->rk', q_rows, key_slab, preferred_element_type=jnp.floa...  23.2 us
    dot_general x16, matrix products, tile_terms(): jnp.einsum('rd,kd->rk', dout_rows, value_slab, preferred_element_type=jnp...  21.8 us
    unnamed x4, waiting for transfers between devices  19 us
  transfers between devices with their start and end apart: 3, of which 3 were waited for; matrix products, arithmetic and copies ran while one was open for 8% of the time, Pallas kernels for 0%

commit v1 on v0

v1 whole, which is shorter than its diff:
```python
from functools import partial
import math

import jax
import jax.numpy as jnp
from jax import lax
from jax.experimental import pallas as pl
from jax.experimental.pallas import tpu as pltpu
from jax.sharding import PartitionSpec as P

BLK = 128
BLK_DEV = 8

NN = (((1,), (0,)), ((), ()))
NT = (((1,), (1,)), ((), ()))


def mm(a, b, dims):
    return lax.dot_general(a, b, dims, preferred_element_type=jnp.float32)


def backward_kernel(
    first_question,
    factor,
    lists,
    place,
    q_ref,
    o_ref,
    do_ref,
    lse_ref,
    k_ref,
    v_ref,
    dq_ref,
    dk_ref,
    dv_ref,
    dk_acc,
    dv_acc,
    kt,
    dqt,
    dq_rows,
):
    step = pl.program_id(0)
    question = step + first_question
    width = k_ref.shape[-1]
    ctx_me, pb_me = place[0], place[1]

    @pl.when(step == 0)
    def _():
        dk_acc[...] = jnp.zeros_like(dk_acc)
        dv_acc[...] = jnp.zeros_like(dv_acc)
        for b in range(BLK_DEV):
            kt[b] = k_ref[b].T

    first_block = ctx_me * BLK_DEV
    start = jnp.int32(0)
    stop = jnp.int32(0)
    for entry in range(lists.shape[1]):
        block = lists[question, entry]
        start += jnp.where((block >= 0) & (block < first_block), 1, 0)
        stop += jnp.where((block >= 0) & (block < first_block + BLK_DEV), 1, 0)
    count = stop - start

    q = q_ref[0]
    do = do_ref[0]
    product = do.astype(jnp.float32) * o_ref[0].astype(jnp.float32)
    high = product.astype(jnp.bfloat16)
    low = (product - high.astype(jnp.float32)).astype(jnp.bfloat16)
    ones = jnp.ones((8, width), jnp.bfloat16)
    delta = (mm(ones, high, NT) + mm(ones, low, NT))[0:1]
    lse = lse_ref[0] * math.log2(math.e)
    scale = factor * math.log2(math.e)
    dqt[...] = jnp.zeros_like(dqt)

    def tiles(blocks):
        keys = jnp.concatenate([k_ref[b] for b in blocks], axis=0)
        values = jnp.concatenate([v_ref[b] for b in blocks], axis=0)
        keys_t = jnp.concatenate([kt[b] for b in blocks], axis=1)
        prob = jnp.exp2(mm(keys, q, NT) * scale - lse)
        dscore = (prob * (mm(values, do, NT) - delta)).astype(jnp.bfloat16)
        dv = mm(prob.astype(jnp.bfloat16), do, NN)
        dk = mm(dscore, q, NN)
        dqt[...] += mm(keys_t, dscore, NN)
        for i, b in enumerate(blocks):
            dv_acc[b] += dv[i * BLK : (i + 1) * BLK]
            dk_acc[b] += dk[i * BLK : (i + 1) * BLK]

    def pair(i, carry):
        at = start + 2 * i
        tiles([lists[question, at] - first_block, lists[question, at + 1] - first_block])
        return carry

    lax.fori_loop(0, count // 2, pair, 0)

    @pl.when(count % 2 == 1)
    def _():
        tiles([lists[question, stop - 1] - first_block])

    dq_rows[...] = dqt[...].T * factor
    parts, rows = dq_ref.shape[0], dq_ref.shape[2]
    for j in range(parts):
        at = pl.multiple_of((ctx_me ^ j) * rows, rows)
        dq_ref[j, 0] = dq_rows[pl.ds(at, rows)]

    @pl.when(step == pl.num_programs(0) - 1)
    def _():
        parts, rows = dk_ref.shape[0], dk_ref.shape[1]
        per = BLK // rows
        for j in range(parts):
            dest = pb_me ^ j
            at = pl.multiple_of((dest % per) * rows, rows)
            dk_ref[j] = dk_acc[dest // per, pl.ds(at, rows)] * factor
            dv_ref[j] = dv_acc[dest // per, pl.ds(at, rows)]


def backward(lists, place, queries, outputs, grads, lse, keys, values, ctx_size, pb_size, first_question, count):
    _, rows, width = queries.shape
    factor = width ** (-0.5)
    local_keys = keys.shape[0] * keys.shape[1]
    per_question = lambda i, *_: (i + first_question, 0, 0)
    whole = lambda i, *_: (0, 0, 0)
    question_spec = pl.BlockSpec((1, rows, width), per_question)
    key_spec = pl.BlockSpec(keys.shape, whole)
    grad_shape = (pb_size, local_keys // pb_size, width)
    dq_shape = (ctx_size, count, rows // ctx_size, width)
    return pl.pallas_call(
        partial(backward_kernel, first_question, factor),
        grid_spec=pltpu.PrefetchScalarGridSpec(
            num_scalar_prefetch=2,
            grid=(count,),
            in_specs=[
                question_spec,
                question_spec,
                question_spec,
                pl.BlockSpec((1, 1, rows), per_question),
                key_spec,
                key_spec,
            ],
            out_specs=[
                pl.BlockSpec((ctx_size, 1, rows // ctx_size, width), lambda i, *_: (0, i, 0, 0)),
                pl.BlockSpec(grad_shape, whole),
                pl.BlockSpec(grad_shape, whole),
            ],
            scratch_shapes=[
                pltpu.VMEM(keys.shape, jnp.float32),
                pltpu.VMEM(keys.shape, jnp.float32),
                pltpu.VMEM((keys.shape[0], width, BLK), jnp.bfloat16),
                pltpu.VMEM((width, rows), jnp.float32),
                pltpu.VMEM((rows, width), jnp.float32),
            ],
        ),
        out_shape=[
            jax.ShapeDtypeStruct(dq_shape, jnp.float32),
            jax.ShapeDtypeStruct(grad_shape, jnp.float32),
            jax.ShapeDtypeStruct(grad_shape, jnp.float32),
        ],
        compiler_params=pltpu.CompilerParams(vmem_limit_bytes=40 * 1024 * 1024),
        cost_estimate=pl.CostEstimate(
            flops=count * rows * local_keys * width * 5, bytes_accessed=count * rows * width * 12, transcendentals=0
        ),
        name="attention_backward",
    )(lists, place, queries, outputs, grads, lse, keys, values)


def swap(array, axis, size, bit):
    return lax.ppermute(array, axis, [(i, i ^ bit) for i in range(size)])


def halving(parts, axis, size, bits):
    for bit in bits:
        kept = [j for j in parts if not j & bit]
        sent = swap(jnp.stack([parts[j | bit] for j in kept]), axis, size, bit)
        parts = {j: parts[j] + sent[i] for i, j in enumerate(kept)}
    return parts[0]


def local(ctx_size, pb_size, queries, keys, values, outputs_saved, grad_out, saved_lse, block_lists):
    questions, tokens, heads, width = queries.shape
    rows = tokens * heads
    flat = lambda a: a.reshape(questions, rows, width)
    blocked = lambda a: a.reshape(BLK_DEV, BLK, width)
    place = jnp.stack([lax.axis_index("ctx"), lax.axis_index("pb")]).astype(jnp.int32)
    dq, dk, dv = backward(
        block_lists,
        place,
        flat(queries),
        flat(outputs_saved),
        flat(grad_out),
        saved_lse.reshape(questions, 1, rows),
        blocked(keys),
        blocked(values),
        ctx_size,
        pb_size,
        0,
        questions,
    )
    ctx_bits = [1 << i for i in range(ctx_size.bit_length() - 1)]
    pb_bits = [1 << i for i in range(pb_size.bit_length() - 1)]
    query_grad = halving({j: dq[j] for j in range(ctx_size)}, "ctx", ctx_size, ctx_bits)
    both = jnp.concatenate([dk, dv], axis=1)
    both = halving({j: both[j] for j in range(pb_size)}, "pb", pb_size, pb_bits)
    half = both.shape[0] // 2
    return (
        query_grad.reshape(questions, tokens // ctx_size, heads, width),
        both[:half],
        both[half:],
    )


def solution(mesh):
    ctx_size, pb_size = mesh.shape["ctx"], mesh.shape["pb"]
    placed = (
        P("pb", None, None, None),
        P("ctx", None),
        P("ctx", None),
        P("pb", None, None, None),
        P("pb", None, None, None),
        P("pb", None, None),
        P("pb", None),
    )
    return jax.shard_map(
        partial(local, ctx_size, pb_size),
        mesh=mesh,
        in_specs=placed,
        out_specs=(P("pb", "ctx", None, None), P(("ctx", "pb"), None), P(("ctx", "pb"), None)),
        check_vma=False,
    )
```

time: 372 us -> 77.2 us (0.21)
  matrix products: 144 us -> 0 us
  waiting for transfers between devices: 148 us -> 33.1 us
  other arithmetic: 31.2 us -> 1.7 us
  local copies, waits for them, and re-layouts: 32.7 us -> 9.44 us
  Pallas kernels: 0 us -> 19.6 us
  between operations: 13.9 us -> 0.74 us
  starting transfers between devices: 0.12 us -> 12.4 us
    dot_general x80 -> x0, matrix products: 144 us -> none  [the longest x16 33.1 us: question_step(): jnp.einsum('rk,rd->kd', prob_tile.astype(jnp.bfloat16), dout_rows, prefer...]
    reduce_scatter x2 -> x0, waiting for transfers between devices: 129 us -> none  [the longest x1 64.9 us: local(): lax.psum_scatter(value_acc.reshape(-1, head_width), 'pb', scatter_dimensi...]
    ppermute x0 -> x5, waiting for transfers between devices: none -> 33.1 us  [swap(): return lax.ppermute(array, axis, [(i, i ^ bit) for i in range(size)])]
    scatter-add x2 -> x0, other arithmetic: 26.4 us -> none  [the longest x1 13.2 us: local(): zero_acc.at[flat_chosen].add(key_parts.reshape(-1, block_rows, head_width))]
    pallas_call x0 -> x1, Pallas kernels: none -> 19.6 us  [backward(): pl.pallas_call(partial(backward_kernel, first_question, factor), grid_spe...]
    unnamed x4 -> x0, waiting for transfers between devices: 19 us -> none
    dynamic_slice x64 -> x0, local copies, waits for them, and re-layouts: 13 us -> none  [local(): lax.scan(stepper, 0, scanned)]
    ppermute x0 -> x5, starting transfers between devices: none -> 12.4 us  [swap(): return lax.ppermute(array, axis, [(i, i ^ bit) for i in range(size)])]
  transfers between devices with their start and end apart: 3 -> 5, of which waited for: 3 -> 4; matrix products, arithmetic and copies ran while one was open for 8% -> 1% of each run, Pallas kernels for 0% -> 0%
where the time goes in v1:
time: 77.2 us; the launch traced here: 77 us
  waiting for transfers between devices  33.1 us (43%)
  Pallas kernels  19.6 us (25%)
  starting transfers between devices  12.4 us (16%)
  local copies, waits for them, and re-layouts  9.44 us (12%)
  other arithmetic  1.7 us (2%)
    ppermute x5, waiting for transfers between devices, swap(): return lax.ppermute(array, axis, [(i, i ^ bit) for i in range(size)])  33.1 us
    pallas_call x1, Pallas kernels, backward(): pl.pallas_call(partial(backward_kernel, first_question, factor), grid_spe...  19.6 us
    ppermute x5, starting transfers between devices, swap(): return lax.ppermute(array, axis, [(i, i ^ bit) for i in range(size)])  12.4 us
    unnamed x14, local copies, waits for them, and re-layouts  8.4 us
  transfers between devices with their start and end apart: 5, of which 4 were waited for; matrix products, arithmetic and copies ran while one was open for 1% of the time, Pallas kernels for 0%

profile of v1, /device:TPU:0, one launch (start us, length us, event | category | flops | bytes accessed | tf_op | source)
XLA Modules:
  0.0 77.0 jit_solution(2852741370242955434)
XLA Ops:
  0.6 1.0 %copy.11 = f32[16,64,8]{0,2,1:T(8,128)S(1)} copy(f32[16,64,8]{1,2,0:T(8,128)} %param.12) | data formatting | bytes 65536 | tf_op args[5]
  1.6 0.1 copy.12.lse_ref
  1.7 0.1 pad_add_fusion.place
  1.8 0.0 copy-start
  1.8 1.6 %copy-done = bf16[16,64,8,128]{3,2,1,0:T(8,128)(2,1)S(1)} copy-done((bf16[16,64,8,128]{3,2,1,0:T(8,128)(2,1)S(1)}, bf16[16,64,8,128]{3,2,1,0:T(8,128)(2,1)}, u32[]{:S(2)}) %copy-start) | copy-done | bytes 2097176
  3.4 0.0 copy-start.1
  3.4 1.6 %copy-done.1 = bf16[16,64,8,128]{3,2,1,0:T(8,128)(2,1)S(1)} copy-done((bf16[16,64,8,128]{3,2,1,0:T(8,128)(2,1)S(1)}, bf16[16,64,8,128]{3,2,1,0:T(8,128)(2,1)}, u32[]{:S(2)}) %copy-start.1) | copy-done | bytes 2097176
  5.0 0.0 copy-start.2
  5.0 1.6 %copy-done.2 = bf16[16,64,8,128]{3,2,1,0:T(8,128)(2,1)S(1)} copy-done((bf16[16,64,8,128]{3,2,1,0:T(8,128)(2,1)S(1)}, bf16[16,64,8,128]{3,2,1,0:T(8,128)(2,1)}, u32[]{:S(2)}) %copy-start.2) | copy-done | bytes 2097176
  6.6 0.0 copy-start.3
  6.6 0.9 %copy-done.3 = bf16[1024,128]{1,0:T(8,128)(2,1)S(1)} copy-done((bf16[1024,128]{1,0:T(8,128)(2,1)S(1)}, bf16[1024,128]{1,0:T(8,128)(2,1)}, u32[]{:S(2)}) %copy-start.3) | copy-done | bytes 262168
  7.5 0.0 copy-start.4
  7.5 0.9 %copy-done.4 = bf16[1024,128]{1,0:T(8,128)(2,1)S(1)} copy-done((bf16[1024,128]{1,0:T(8,128)(2,1)S(1)}, bf16[1024,128]{1,0:T(8,128)(2,1)}, u32[]{:S(2)}) %copy-start.4) | copy-done | bytes 262168
  8.5 0.0 copy-start.5
  8.5 0.7 copy-done.5
  9.2 19.6 %attention_backward.1 = (f32[4,16,128,128]{3,2,1,0:T(8,128)S(1)}, f32[8,128,128]{2,1,0:T(8,128)S(1)}, f32[8,128,128]{2,1,0:T(8,128)S(1)}) custom-call(s32[16,24]{1,0:T(8,128)S(1)} %copy-done.5, s32[2]{0:T(128)S(1)} %pad_add_fusion.place, bf16[16,512,128]{2,1,0:T(8,128)(2,1)S(1)} %bitcast.14, bf16[16,512,128]{2,1,0:T(8,128)(2,1)S(1)} %bitcast.15, ...), custom_call_target="tpu_custom_call" | custom-call | flops 5368709120 | bytes 12582912 | tf_op jit(solution)/shard_map/attention_backward/pallas_call | solution.py:125
  28.8 0.2 fusion.3
  29.1 0.2 pad_maximum_fusion
  29.3 5.7 %collective-permute-start = (f32[2,16,128,128]{3,2,1,0:T(8,128)S(1)}, f32[2,16,128,128]{3,2,1,0:T(8,128)S(1)}, u32[]{:S(2)}, u32[]{:S(2)}) collective-permute-start(f32[2,16,128,128]{3,2,1,0:T(8,128)S(1)} %pad_maximum_fusion), channel_id=1, source_target_pairs={{0,8},{8,0},{16,24},{24,16},{1,9},{9,1},{17,25},{25,17},{2,10},{10... | collective-permute-start | bytes 6291464 | tf_op jit(solution)/shard_map/ppermute | solution.py:165
  35.2 0.1 collective-permute-start.2
  35.3 13.8 %collective-permute-done.2 = f32[4,256,128]{2,1,0:T(8,128)S(1)} collective-permute-done((f32[4,256,128]{2,1,0:T(8,128)S(1)}, f32[4,256,128]{2,1,0:T(8,128)S(1)}, u32[]{:S(2)}, u32[]{:S(2)}) %collective-permute-start.2) | collective-permute-done | bytes 524320 | tf_op jit(solution)/shard_map/ppermute | solution.py:165
  49.2 0.1 collective-permute-start.3
  49.3 0.0 collective-permute-done
  49.3 0.1 slice_add_fusion
  49.4 4.0 %collective-permute-start.1 = (f32[1,16,128,128]{3,2,1,0:T(8,128)S(1)}, f32[1,16,128,128]{3,2,1,0:T(8,128)S(1)}, u32[]{:S(2)}, u32[]{:S(2)}) collective-permute-start(f32[1,16,128,128]{3,2,1,0:T(8,128)S(1)} %slice_add_fusion), channel_id=1, source_target_pairs={{0,16},{8,24},{16,0},{24,8},{1,17},{9,25},{17,1},{25,9},{2,18},{10... | collective-permute-start | bytes 3145736 | tf_op jit(solution)/shard_map/ppermute | solution.py:165
  53.4 3.2 %collective-permute-done.3 = f32[2,256,128]{2,1,0:T(8,128)S(1)} collective-permute-done((f32[2,256,128]{2,1,0:T(8,128)S(1)}, f32[2,256,128]{2,1,0:T(8,128)S(1)}, u32[]{:S(2)}, u32[]{:S(2)}) %collective-permute-start.3) | collective-permute-done | bytes 262176 | tf_op jit(solution)/shard_map/ppermute | solution.py:165
  56.6 2.5 %collective-permute-start.4 = (f32[1,256,128]{2,1,0:T(8,128)S(1)}, f32[1,256,128]{2,1,0:T(8,128)S(1)}, u32[]{:S(2)}, u32[]{:S(2)}) collective-permute-start(f32[1,256,128]{2,1,0:T(8,128)S(1)} %slice_add_fusion.2), channel_id=1, source_target_pairs={{0,4},{1,5},{2,6},{3,7},{4,0},{5,1},{6,2},{7,3},{8,12},{9,13},{10,... | collective-permute-start | bytes 393224 | tf_op jit(solution)/shard_map/ppermute | solution.py:165
  59.2 5.0 %collective-permute-done.4 = f32[1,256,128]{2,1,0:T(8,128)S(1)} collective-permute-done((f32[1,256,128]{2,1,0:T(8,128)S(1)}, f32[1,256,128]{2,1,0:T(8,128)S(1)}, u32[]{:S(2)}, u32[]{:S(2)}) %collective-permute-start.4) | collective-permute-done | bytes 131104 | tf_op jit(solution)/shard_map/ppermute | solution.py:165
  64.2 0.7 slice_bitcast_fusion
  64.8 11.1 %collective-permute-done.1 = f32[1,16,128,128]{3,2,1,0:T(8,128)S(1)} collective-permute-done((f32[1,16,128,128]{3,2,1,0:T(8,128)S(1)}, f32[1,16,128,128]{3,2,1,0:T(8,128)S(1)}, u32[]{:S(2)}, u32[]{:S(2)}) %collective-permute-start.1) | collective-permute-done | bytes 1048608 | tf_op jit(solution)/shard_map/ppermute | solution.py:165
  75.9 1.1 %fusion.1 = f32[16,16,8,128]{3,2,1,0:T(8,128)} fusion(f32[1,16,128,128]{3,2,1,0:T(8,128)S(1)} %collective-permute-done.1, f32[2,16,128,128]{3,2,1,0:T(8,128)S(1)} %collective-permute-done, f32[4,16,128,128]{3,2,1,0:T(8,128)S(1)} %get-tuple-element.6), kind=kLoop, calls=%fused_computation.4 | loop fusion | flops 524288 | bytes 4194304 | tf_op jit(solution)/shard_map/add | solution.py:172
  (8 shorter events, 0.2 us)
Async XLA Ops:
  1.8 1.6 %copy-start = (bf16[16,64,8,128]{3,2,1,0:T(8,128)(2,1)S(1)}, bf16[16,64,8,128]{3,2,1,0:T(8,128)(2,1)}, u32[]{:S(2)}) copy-start(bf16[16,64,8,128]{3,2,1,0:T(8,128)(2,1)} %param.7) | copy-start | bytes 6291460
  3.4 1.6 %copy-start.1 = (bf16[16,64,8,128]{3,2,1,0:T(8,128)(2,1)S(1)}, bf16[16,64,8,128]{3,2,1,0:T(8,128)(2,1)}, u32[]{:S(2)}) copy-start(bf16[16,64,8,128]{3,2,1,0:T(8,128)(2,1)} %param.10) | copy-start | bytes 6291460
  5.0 1.6 %copy-start.2 = (bf16[16,64,8,128]{3,2,1,0:T(8,128)(2,1)S(1)}, bf16[16,64,8,128]{3,2,1,0:T(8,128)(2,1)}, u32[]{:S(2)}) copy-start(bf16[16,64,8,128]{3,2,1,0:T(8,128)(2,1)} %param.11) | copy-start | bytes 6291460
  6.6 0.9 %copy-start.3 = (bf16[1024,128]{1,0:T(8,128)(2,1)S(1)}, bf16[1024,128]{1,0:T(8,128)(2,1)}, u32[]{:S(2)}) copy-start(bf16[1024,128]{1,0:T(8,128)(2,1)} %param.8) | copy-start | bytes 786436
  7.5 0.9 %copy-start.4 = (bf16[1024,128]{1,0:T(8,128)(2,1)S(1)}, bf16[1024,128]{1,0:T(8,128)(2,1)}, u32[]{:S(2)}) copy-start(bf16[1024,128]{1,0:T(8,128)(2,1)} %param.9) | copy-start | bytes 786436
  8.5 0.7 copy-start.5
  29.3 20.0 %collective-permute-start = (f32[2,16,128,128]{3,2,1,0:T(8,128)S(1)}, f32[2,16,128,128]{3,2,1,0:T(8,128)S(1)}, u32[]{:S(2)}, u32[]{:S(2)}) collective-permute-start(f32[2,16,128,128]{3,2,1,0:T(8,128)S(1)} %pad_maximum_fusion), channel_id=1, source_target_pairs={{0,8},{8,0},{16,24},{24,16},{1,9},{9,1},{17,25},{25,17},{2,10},{10... | collective-permute-start | bytes 6291464 | tf_op jit(solution)/shard_map/ppermute | solution.py:165
  35.2 13.9 %collective-permute-start.2 = (f32[4,256,128]{2,1,0:T(8,128)S(1)}, f32[4,256,128]{2,1,0:T(8,128)S(1)}, u32[]{:S(2)}, u32[]{:S(2)}) collective-permute-start(f32[4,256,128]{2,1,0:T(8,128)S(1)} %pad_maximum_fusion.1), channel_id=1, source_target_pairs={{0,1},{1,0},{2,3},{3,2},{4,5},{5,4},{6,7},{7,6},{8,9},{9,8},{10,11... | collective-permute-start | bytes 1572872 | tf_op jit(solution)/shard_map/ppermute | solution.py:165
  49.2 7.4 %collective-permute-start.3 = (f32[2,256,128]{2,1,0:T(8,128)S(1)}, f32[2,256,128]{2,1,0:T(8,128)S(1)}, u32[]{:S(2)}, u32[]{:S(2)}) collective-permute-start(f32[2,256,128]{2,1,0:T(8,128)S(1)} %pad_maximum_fusion.2), channel_id=1, source_target_pairs={{0,2},{1,3},{2,0},{3,1},{4,6},{5,7},{6,4},{7,5},{8,10},{9,11},{10,... | collective-permute-start | bytes 786440 | tf_op jit(solution)/shard_map/ppermute | solution.py:165
  49.4 26.5 %collective-permute-start.1 = (f32[1,16,128,128]{3,2,1,0:T(8,128)S(1)}, f32[1,16,128,128]{3,2,1,0:T(8,128)S(1)}, u32[]{:S(2)}, u32[]{:S(2)}) collective-permute-start(f32[1,16,128,128]{3,2,1,0:T(8,128)S(1)} %slice_add_fusion), channel_id=1, source_target_pairs={{0,16},{8,24},{16,0},{24,8},{1,17},{9,25},{17,1},{25,9},{2,18},{10... | collective-permute-start | bytes 3145736 | tf_op jit(solution)/shard_map/ppermute | solution.py:165
  56.6 7.5 %collective-permute-start.4 = (f32[1,256,128]{2,1,0:T(8,128)S(1)}, f32[1,256,128]{2,1,0:T(8,128)S(1)}, u32[]{:S(2)}, u32[]{:S(2)}) collective-permute-start(f32[1,256,128]{2,1,0:T(8,128)S(1)} %slice_add_fusion.2), channel_id=1, source_target_pairs={{0,4},{1,5},{2,6},{3,7},{4,0},{5,1},{6,2},{7,3},{8,12},{9,13},{10,... | collective-permute-start | bytes 393224 | tf_op jit(solution)/shard_map/ppermute | solution.py:165

commit v2 on v0

v2 whole, which is shorter than its diff:
```python
from functools import partial
import math

import jax
import jax.numpy as jnp
from jax import lax
from jax.experimental import pallas as pl
from jax.experimental.pallas import tpu as pltpu
from jax.sharding import PartitionSpec as P

BLK = 128
BLK_DEV = 8
PAIRS = BLK_DEV // 2
NONE = BLK_DEV

NN = (((1,), (0,)), ((), ()))
NT = (((1,), (1,)), ((), ()))
TN = (((0,), (0,)), ((), ()))


def mm(a, b, dims):
    return lax.dot_general(a, b, dims, preferred_element_type=jnp.float32)


def backward_kernel(first, count, factor, has_prior, has_after, *refs):
    lists_hbm, lse_hbm, q_hbm, o_hbm, do_hbm, k_hbm, v_hbm = refs[:7]
    refs = refs[7:]
    prior = refs[:2] if has_prior else None
    refs = refs[2:] if has_prior else refs
    refs = refs[1:] if has_after else refs
    dq_ref, dk_ref, dv_ref = refs[:3]
    q_all, o_all, do_all, k_all, v_all, lse_all, delta_all, dk_acc, dv_acc = refs[3:12]
    prob0, prob1, ds0, ds1, lse_ref, lists, items, sems = refs[12:]
    prob_slots, ds_slots = (prob0, prob1), (ds0, ds1)
    rows, width = q_all.shape[1], q_all.shape[2]
    ctx_me, pb_me = lax.axis_index("ctx"), lax.axis_index("pb")

    mine = pl.ds(first, count)
    copies = [
        pltpu.make_async_copy(src, dst, sems.at[n])
        for n, (src, dst) in enumerate(
            (
                (lists_hbm, lists),
                (lse_hbm.at[mine], lse_ref),
                (do_hbm.at[mine], do_all),
                (o_hbm.at[mine], o_all),
                (q_hbm.at[mine], q_all),
                (k_hbm, k_all.at[pl.ds(0, BLK_DEV)]),
                (v_hbm, v_all.at[pl.ds(0, BLK_DEV)]),
            )
        )
    ]
    for copy in copies:
        copy.start()

    dq_ref[...] = jnp.zeros_like(dq_ref)
    dk_acc[...] = jnp.zeros_like(dk_acc)
    dv_acc[...] = jnp.zeros_like(dv_acc)
    k_all[NONE] = jnp.zeros((BLK, width), k_all.dtype)
    v_all[NONE] = jnp.zeros((BLK, width), v_all.dtype)

    copies[0].wait()
    first_block = ctx_me * BLK_DEV
    below, above = first_block.astype(jnp.uint32), (first_block + BLK_DEV).astype(jnp.uint32)
    last = lists.shape[1] - 1
    total = jnp.int32(0)
    for i in range(count):
        start = jnp.int32(0)
        stop = jnp.int32(0)
        for entry in range(last + 1):
            block = lists[first + i, entry].astype(jnp.uint32)
            start += (block < below).astype(jnp.int32)
            stop += (block < above).astype(jnp.int32)
        for p in range(PAIRS):
            at = start + 2 * p
            items[0, total + p] = i
            items[1, total + p] = lists[first + i, jnp.minimum(at, last)] - first_block
            items[2, total + p] = jnp.where(
                at + 1 < stop, lists[first + i, jnp.minimum(at + 1, last)] - first_block, NONE
            )
        total += (stop - start + 1) // 2
    for p in range(2):
        items[0, total + p] = 0
        items[1, total + p] = NONE
        items[2, total + p] = NONE

    copies[1].wait()
    heads, tokens = lse_ref.shape[1], lse_ref.shape[2]
    lse_rest = lse_ref[...].reshape(count * heads, tokens) * math.log2(math.e)
    row = lax.broadcasted_iota(jnp.int32, (tokens, rows), 1) // heads
    spread = (row == lax.broadcasted_iota(jnp.int32, (tokens, rows), 0)).astype(jnp.bfloat16)
    lse_rows = jnp.zeros((count * heads, rows), jnp.float32)
    for _ in range(3):
        piece = lse_rest.astype(jnp.bfloat16)
        lse_rest = lse_rest - piece.astype(jnp.float32)
        lse_rows += mm(piece, spread, NN)
    head_of_row = lax.broadcasted_iota(jnp.int32, (heads, rows), 1) % heads
    own_head = head_of_row == lax.broadcasted_iota(jnp.int32, (heads, rows), 0)
    for i in range(count):
        picked = jnp.where(own_head, lse_rows[i * heads : (i + 1) * heads], 0.0)
        lse_all[i] = jnp.sum(picked, axis=0, keepdims=True)

    for copy in copies[2:]:
        copy.wait()
    ones = jnp.ones((8, 2 * width), jnp.bfloat16)
    for i in range(count):
        product = do_all[i].astype(jnp.float32) * o_all[i].astype(jnp.float32)
        high = product.astype(jnp.bfloat16)
        low = (product - high.astype(jnp.float32)).astype(jnp.bfloat16)
        delta_all[i] = mm(ones, jnp.concatenate([high, low], axis=1), NT)[0:1]

    scale = factor * math.log2(math.e)
    parts, part_rows = dq_ref.shape[0], dq_ref.shape[2]

    def scores(item, slot):
        i, b0, b1 = items[0, item], items[1, item], items[2, item]
        keys = jnp.concatenate([k_all[b0], k_all[b1]], axis=0)
        values = jnp.concatenate([v_all[b0], v_all[b1]], axis=0)
        prob = jnp.exp2(mm(keys, q_all[i], NT) * scale - lse_all[i])
        dprob = mm(values, do_all[i], NT)
        prob_slots[slot][...] = prob.astype(jnp.bfloat16)
        ds_slots[slot][...] = (prob * (dprob - delta_all[i])).astype(jnp.bfloat16)

    def gradients(item, slot):
        i, b0, b1 = items[0, item], items[1, item], items[2, item]
        keys = jnp.concatenate([k_all[b0], k_all[b1]], axis=0)
        dscore = ds_slots[slot][...]
        dv = mm(prob_slots[slot][...], do_all[i], NN)
        dk = mm(dscore, q_all[i], NN)
        dq = mm(dscore, keys, TN) * factor
        for j in range(parts):
            dq_ref[ctx_me ^ j, i] += dq[j * part_rows : (j + 1) * part_rows]
        dv_acc[b0] += dv[:BLK]
        dk_acc[b0] += dk[:BLK]
        dv_acc[b1] += dv[BLK:]
        dk_acc[b1] += dk[BLK:]

    scores(0, 0)

    def two_items(step, carry):
        scores(2 * step + 1, 1)
        gradients(2 * step, 0)
        scores(2 * step + 2, 0)
        gradients(2 * step + 1, 1)
        return carry

    lax.fori_loop(0, (total + 1) // 2, two_items, 0)

    parts, part_rows = dk_ref.shape[0], dk_ref.shape[1]
    per = BLK // part_rows
    for j in range(parts):
        dest = pb_me ^ j
        at = pl.multiple_of((dest % per) * part_rows, part_rows)
        dk = dk_acc[dest // per, pl.ds(at, part_rows)] * factor
        dv = dv_acc[dest // per, pl.ds(at, part_rows)]
        dk_ref[j] = dk + prior[0][j] if has_prior else dk
        dv_ref[j] = dv + prior[1][j] if has_prior else dv


def backward(lists, lse, queries, outputs, grads, keys, values, sizes, first, count, prior=(), after=()):
    ctx_size, pb_size = sizes
    _, rows, width = queries.shape
    heads = lse.shape[1]
    local_keys = keys.shape[0] * keys.shape[1]
    grad_shape = (pb_size, local_keys // pb_size, width)
    dq_shape = (ctx_size, count, rows // ctx_size, width)
    vmem = pl.BlockSpec(memory_space=pltpu.VMEM)
    hbm = pl.BlockSpec(memory_space=pltpu.HBM)
    f32, bf16 = jnp.float32, jnp.bfloat16
    in_hbm = [pltpu.with_memory_space_constraint(a, pltpu.HBM) for a in (lists, lse, queries, outputs, grads, keys, values)]
    return pl.pallas_call(
        partial(backward_kernel, first, count, width ** (-0.5), bool(prior), bool(after)),
        in_specs=[hbm] * 7 + [vmem] * len(prior) + [pl.BlockSpec(memory_space=pl.ANY)] * len(after),
        out_specs=[vmem] * 3,
        out_shape=[
            pltpu.VMEM(dq_shape, f32),
            pltpu.VMEM(grad_shape, f32),
            pltpu.VMEM(grad_shape, f32),
        ],
        scratch_shapes=[
            pltpu.VMEM((count, rows, width), bf16),
            pltpu.VMEM((count, rows, width), bf16),
            pltpu.VMEM((count, rows, width), bf16),
            pltpu.VMEM((BLK_DEV + 1, BLK, width), bf16),
            pltpu.VMEM((BLK_DEV + 1, BLK, width), bf16),
            pltpu.VMEM((count, 1, rows), f32),
            pltpu.VMEM((count, 1, rows), f32),
            pltpu.VMEM((BLK_DEV + 1, BLK, width), f32),
            pltpu.VMEM((BLK_DEV + 1, BLK, width), f32),
            pltpu.VMEM((2 * BLK, rows), bf16),
            pltpu.VMEM((2 * BLK, rows), bf16),
            pltpu.VMEM((2 * BLK, rows), bf16),
            pltpu.VMEM((2 * BLK, rows), bf16),
            pltpu.VMEM((count,) + lse.shape[1:], f32),
            pltpu.SMEM(lists.shape, jnp.int32),
            pltpu.SMEM((3, (count + 1) * PAIRS), jnp.int32),
            pltpu.SemaphoreType.DMA((7,)),
        ],
        compiler_params=pltpu.CompilerParams(vmem_limit_bytes=32 * 1024 * 1024),
        cost_estimate=pl.CostEstimate(
            flops=count * rows * local_keys * width * 5, bytes_accessed=count * rows * width * 12, transcendentals=0
        ),
        name="attention_backward",
    )(*in_hbm, *prior, *after)


def swap(array, axis, size, bit):
    return lax.ppermute(array, axis, [(i, i ^ bit) for i in range(size)])


def exchange(groups, axis, size, bit):
    sent = jnp.stack([parts[j] for parts in groups for j in sorted(parts) if j & bit])
    got = iter(swap(sent, axis, size, bit))
    return [{j: parts[j] + next(got) for j in sorted(parts) if not j & bit} for parts in groups]


def bits_of(size):
    return [1 << i for i in range(size.bit_length() - 1)]


def sum_two_ways(first, second, axis, size, after):
    order = bits_of(size)
    other = order[1::-1] + order[2:]
    for one, two in zip(order, other):
        if one == two:
            first, second = exchange([first, second], axis, size, one)
        else:
            (first,) = exchange([first], axis, size, one)
            (second,) = exchange([second], axis, size, two)
    return first[0], second[0]


def local(ctx_size, pb_size, queries, keys, values, outputs_saved, grad_out, saved_lse, block_lists):
    questions, tokens, heads, width = queries.shape
    rows = tokens * heads
    flat = lambda a: a.reshape(questions, rows, width)
    blocked = lambda a: a.reshape(BLK_DEV, BLK, width)
    run = partial(
        backward,
        block_lists,
        jnp.swapaxes(saved_lse, 1, 2),
        flat(queries),
        flat(outputs_saved),
        flat(grad_out),
        blocked(keys),
        blocked(values),
        (ctx_size, pb_size),
    )
    early = questions * 9 // 16
    core, rest = bits_of(ctx_size)[0], bits_of(ctx_size)[1:]
    by_dest = lambda a: {j: a[j] for j in range(a.shape[0])}

    def across(parts):
        for bit in rest:
            (parts,) = exchange([parts], "ctx", ctx_size, bit)
        return parts[0]

    dq, dk, dv = run(0, early)
    (parts,) = exchange([by_dest(dq)], "ctx", ctx_size, core)
    early_grad = across(parts)
    dq, dk, dv = run(early, questions - early, (dk, dv), (parts[2],))
    dq, early_grad = lax.optimization_barrier((dq, early_grad))
    (parts,) = exchange([by_dest(dq)], "ctx", ctx_size, core)
    key_grad, value_grad = sum_two_ways(by_dest(dk), by_dest(dv), "pb", pb_size, parts)
    mine, key_grad, value_grad = lax.optimization_barrier((parts[0], key_grad, value_grad))
    parts = {**parts, 0: mine}
    late_grad = across(parts)
    done = [early_grad, late_grad]
    query_grad = jnp.concatenate(done, axis=0)
    return query_grad.reshape(questions, tokens // ctx_size, heads, width), key_grad, value_grad


def solution(mesh):
    ctx_size, pb_size = mesh.shape["ctx"], mesh.shape["pb"]
    placed = (
        P("pb", None, None, None),
        P("ctx", None),
        P("ctx", None),
        P("pb", None, None, None),
        P("pb", None, None, None),
        P("pb", None, None),
        P("pb", None),
    )
    return jax.shard_map(
        partial(local, ctx_size, pb_size),
        mesh=mesh,
        in_specs=placed,
        out_specs=(P("pb", "ctx", None, None), P(("ctx", "pb"), None), P(("ctx", "pb"), None)),
        check_vma=False,
    )
```

time: 372 us -> 55.7 us (0.15)
  matrix products: 144 us -> 0 us
  waiting for transfers between devices: 148 us -> 20.6 us
  local copies, waits for them, and re-layouts: 32.7 us -> 0.21 us
  other arithmetic: 31.2 us -> 2.32 us
  Pallas kernels: 0 us -> 15.6 us
  starting transfers between devices: 0.12 us -> 15.5 us
  between operations: 13.9 us -> 0.79 us
    dot_general x80 -> x0, matrix products: 144 us -> none  [the longest x16 33.1 us: question_step(): jnp.einsum('rk,rd->kd', prob_tile.astype(jnp.bfloat16), dout_rows, prefer...]
    reduce_scatter x2 -> x0, waiting for transfers between devices: 129 us -> none  [the longest x1 64.9 us: local(): lax.psum_scatter(value_acc.reshape(-1, head_width), 'pb', scatter_dimensi...]
    scatter-add x2 -> x0, other arithmetic: 26.4 us -> none  [the longest x1 13.2 us: local(): zero_acc.at[flat_chosen].add(key_parts.reshape(-1, block_rows, head_width))]
    ppermute x0 -> x9, waiting for transfers between devices: none -> 20.6 us  [swap(): return lax.ppermute(array, axis, [(i, i ^ bit) for i in range(size)])]
    unnamed x4 -> x0, waiting for transfers between devices: 19 us -> none
    pallas_call x0 -> x2, Pallas kernels: none -> 15.6 us  [backward(): pl.pallas_call(partial(backward_kernel, first, count, width ** (-0.5), bo...]
    ppermute x0 -> x9, starting transfers between devices: none -> 15.5 us  [swap(): return lax.ppermute(array, axis, [(i, i ^ bit) for i in range(size)])]
    dynamic_slice x64 -> x0, local copies, waits for them, and re-layouts: 13 us -> none  [local(): lax.scan(stepper, 0, scanned)]
  transfers between devices with their start and end apart: 3 -> 9, of which waited for: 3 -> 8; matrix products, arithmetic and copies ran while one was open for 8% -> 2% of each run, Pallas kernels for 0% -> 15%
where the time goes in v2:
time: 55.7 us; the launch traced here: 55 us
  waiting for transfers between devices  20.6 us (37%)
  Pallas kernels  15.6 us (28%)
  starting transfers between devices  15.5 us (28%)
  other arithmetic  2.32 us (4%)
  between operations  0.79 us (1%)
    ppermute x9, waiting for transfers between devices, swap(): return lax.ppermute(array, axis, [(i, i ^ bit) for i in range(size)])  20.6 us
    pallas_call x2, Pallas kernels, backward(): pl.pallas_call(partial(backward_kernel, first, count, width ** (-0.5), bo...  15.6 us
    ppermute x9, starting transfers between devices, swap(): return lax.ppermute(array, axis, [(i, i ^ bit) for i in range(size)])  15.5 us
  transfers between devices with their start and end apart: 9, of which 8 were waited for; matrix products, arithmetic and copies ran while one was open for 2% of the time, Pallas kernels for 15%

profile of v2, /device:TPU:0, one launch (start us, length us, event | category | flops | bytes accessed | tf_op | source)
XLA Modules:
  0.0 55.0 jit_solution(6099824605575782329)
XLA Ops:
  0.6 7.5 %attention_backward.2 = (f32[4,9,128,128]{3,2,1,0:T(8,128)S(1)}, f32[8,128,128]{2,1,0:T(8,128)S(1)}, f32[8,128,128]{2,1,0:T(8,128)S(1)}) custom-call(s32[16,24]{1,0:T(8,128)} %refs_0_.3, f32[16,8,64]{2,1,0:T(8,128)} %bitcast.30, bf16[16,512,128]{2,1,0:T(8,128)(2,1)} %bitcast.20, bf16[16,512,128]{2,1,0:T(8,128)(2,1)} %bitcast.22, ...), custom_call_target="tpu_custom_call" | custom-call | flops 3019898880 | bytes 7077888 | tf_op jit(solution)/shard_map/attention_backward/pallas_call | solution.py:171
  8.2 0.1 fusion.5
  8.3 0.1 pad_maximum_fusion
  8.4 0.1 collective-permute-start
  8.5 2.8 %collective-permute-done = f32[2,9,128,128]{3,2,1,0:T(8,128)S(1)} collective-permute-done((f32[2,9,128,128]{3,2,1,0:T(8,128)S(1)}, f32[2,9,128,128]{3,2,1,0:T(8,128)S(1)}, u32[]{:S(2)}, u32[]{:S(2)}) %collective-permute-start) | collective-permute-done | bytes 1179680 | tf_op jit(solution)/shard_map/ppermute | solution.py:208
  11.3 0.1 slice_add_fusion.1
  11.4 8.6 %collective-permute-start.1 = (f32[1,9,128,128]{3,2,1,0:T(8,128)S(1)}, f32[1,9,128,128]{3,2,1,0:T(8,128)S(1)}, u32[]{:S(2)}, u32[]{:S(2)}) collective-permute-start(f32[1,9,128,128]{3,2,1,0:T(8,128)S(1)} %slice_add_fusion.1), channel_id=1, source_target_pairs={{0,16},{8,24},{16,0},{24,8},{1,17},{9,25},{17,1},{25,9},{2,18},{10... | collective-permute-start | bytes 1769480 | tf_op jit(solution)/shard_map/ppermute | solution.py:208
  19.9 8.1 %attention_backward.3 = (f32[4,7,128,128]{3,2,1,0:T(8,128)S(1)}, f32[8,128,128]{2,1,0:T(8,128)S(1)}, f32[8,128,128]{2,1,0:T(8,128)S(1)}) custom-call(s32[16,24]{1,0:T(8,128)} %refs_0_.3, f32[16,8,64]{2,1,0:T(8,128)} %bitcast.31, bf16[16,512,128]{2,1,0:T(8,128)(2,1)} %bitcast.21, bf16[16,512,128]{2,1,0:T(8,128)(2,1)} %bitcast.23, ...), custom_call_target="tpu_custom_call" | custom-call | flops 2348810240 | bytes 5505024 | tf_op jit(solution)/shard_map/attention_backward/pallas_call | solution.py:171
  28.1 0.1 collective-permute-start.5
  28.2 2.8 %collective-permute-start.3 = (f32[4,128,128]{2,1,0:T(8,128)S(1)}, f32[4,128,128]{2,1,0:T(8,128)S(1)}, u32[]{:S(2)}, u32[]{:S(2)}) collective-permute-start(f32[4,128,128]{2,1,0:T(8,128)S(1)} %pad_maximum_fusion.2), channel_id=1, source_target_pairs={{0,1},{1,0},{2,3},{3,2},{4,5},{5,4},{6,7},{7,6},{8,9},{9,8},{10,11... | collective-permute-start | bytes 786440 | tf_op jit(solution)/shard_map/ppermute | solution.py:208
  31.0 2.8 %collective-permute-done.1 = f32[1,9,128,128]{3,2,1,0:T(8,128)S(1)} collective-permute-done((f32[1,9,128,128]{3,2,1,0:T(8,128)S(1)}, f32[1,9,128,128]{3,2,1,0:T(8,128)S(1)}, u32[]{:S(2)}, u32[]{:S(2)}) %collective-permute-start.1) | collective-permute-done | bytes 589856 | tf_op jit(solution)/shard_map/ppermute | solution.py:208
  33.8 0.1 fusion.1
  33.9 0.1 fusion.6
  34.0 0.1 pad_maximum_fusion.1
  34.0 0.1 collective-permute-start.2
  34.1 2.3 %collective-permute-done.5 = f32[4,128,128]{2,1,0:T(8,128)S(1)} collective-permute-done((f32[4,128,128]{2,1,0:T(8,128)S(1)}, f32[4,128,128]{2,1,0:T(8,128)S(1)}, u32[]{:S(2)}, u32[]{:S(2)}) %collective-permute-start.5) | collective-permute-done | bytes 262176 | tf_op jit(solution)/shard_map/ppermute | solution.py:208
  36.4 0.1 collective-permute-done.3
  36.6 1.8 %collective-permute-start.4 = (f32[2,128,128]{2,1,0:T(8,128)S(1)}, f32[2,128,128]{2,1,0:T(8,128)S(1)}, u32[]{:S(2)}, u32[]{:S(2)}) collective-permute-start(f32[2,128,128]{2,1,0:T(8,128)S(1)} %pad_maximum_fusion.4), channel_id=1, source_target_pairs={{0,2},{1,3},{2,0},{3,1},{4,6},{5,7},{6,4},{7,5},{8,10},{9,11},{10,... | collective-permute-start | bytes 393224 | tf_op jit(solution)/shard_map/ppermute | solution.py:208
  38.4 0.4 collective-permute-start.6
  38.8 2.9 %collective-permute-done.4 = f32[2,128,128]{2,1,0:T(8,128)S(1)} collective-permute-done((f32[2,128,128]{2,1,0:T(8,128)S(1)}, f32[2,128,128]{2,1,0:T(8,128)S(1)}, u32[]{:S(2)}, u32[]{:S(2)}) %collective-permute-start.4) | collective-permute-done | bytes 131104 | tf_op jit(solution)/shard_map/ppermute | solution.py:208
  41.7 1.8 %collective-permute-done.6 = f32[2,128,128]{2,1,0:T(8,128)S(1)} collective-permute-done((f32[2,128,128]{2,1,0:T(8,128)S(1)}, f32[2,128,128]{2,1,0:T(8,128)S(1)}, u32[]{:S(2)}, u32[]{:S(2)}) %collective-permute-start.6) | collective-permute-done | bytes 131104 | tf_op jit(solution)/shard_map/ppermute | solution.py:208
  43.5 0.0 collective-permute-done.2
  43.5 0.1 slice_add_fusion.2
  43.6 0.4 collective-permute-start.8
  44.0 1.4 %collective-permute-start.7 = (f32[2,128,128]{2,1,0:T(8,128)S(1)}, f32[2,128,128]{2,1,0:T(8,128)S(1)}, u32[]{:S(2)}, u32[]{:S(2)}) collective-permute-start(f32[2,128,128]{2,1,0:T(8,128)S(1)} %pad_maximum_fusion.6), channel_id=1, source_target_pairs={{0,4},{1,5},{2,6},{3,7},{4,0},{5,1},{6,2},{7,3},{8,12},{9,13},{10,... | collective-permute-start | bytes 393224 | tf_op jit(solution)/shard_map/ppermute | solution.py:208
  45.4 5.9 %collective-permute-done.7 = f32[2,128,128]{2,1,0:T(8,128)S(1)} collective-permute-done((f32[2,128,128]{2,1,0:T(8,128)S(1)}, f32[2,128,128]{2,1,0:T(8,128)S(1)}, u32[]{:S(2)}, u32[]{:S(2)}) %collective-permute-start.7) | collective-permute-done | bytes 131104 | tf_op jit(solution)/shard_map/ppermute | solution.py:208
  51.3 0.7 %fusion.3 = (f32[128,128]{1,0:T(8,128)}, f32[128,128]{1,0:T(8,128)}) fusion(f32[2,128,128]{2,1,0:T(8,128)S(1)} %collective-permute-done.7, f32[2,128,128]{2,1,0:T(8,128)S(1)} %collective-permute-done.6, f32[4,128,128]{2,1,0:T(8,128)S(1)} %collective-permute-done.5, f32[8,128,128]{2,1,0:T(8,128)S(1)} %get-tuple-element.21, ...), kind=kLoop, calls=%fused_computation.17 | loop fusion | flops 98304 | bytes 655360 | tf_op jit(solution)/shard_map/add | solution.py:214
  52.0 1.9 %collective-permute-done.8 = f32[1,7,128,128]{3,2,1,0:T(8,128)S(1)} collective-permute-done((f32[1,7,128,128]{3,2,1,0:T(8,128)S(1)}, f32[1,7,128,128]{3,2,1,0:T(8,128)S(1)}, u32[]{:S(2)}, u32[]{:S(2)}) %collective-permute-start.8) | collective-permute-done | bytes 458784 | tf_op jit(solution)/shard_map/ppermute | solution.py:208
  53.8 0.1 bitcast_add_fusion
  53.9 1.0 %maximum_bitcast_fusion = f32[16,16,8,128]{3,2,1,0:T(8,128)} fusion(f32[7,128,128]{2,1,0:T(8,128)S(1)} %bitcast_add_fusion, f32[9,128,128]{2,1,0:T(8,128)S(1)} %fusion.1), kind=kLoop, calls=%fused_computation.1 | loop fusion | flops 262144 | bytes 2097152 | tf_op jit(solution)/shard_map/reshape | solution.py:270
  (10 shorter events, 0.2 us)
Async XLA Ops:
  8.4 2.9 %collective-permute-start = (f32[2,9,128,128]{3,2,1,0:T(8,128)S(1)}, f32[2,9,128,128]{3,2,1,0:T(8,128)S(1)}, u32[]{:S(2)}, u32[]{:S(2)}) collective-permute-start(f32[2,9,128,128]{3,2,1,0:T(8,128)S(1)} %pad_maximum_fusion), channel_id=1, source_target_pairs={{0,8},{8,0},{16,24},{24,16},{1,9},{9,1},{17,25},{25,17},{2,10},{10... | collective-permute-start | bytes 3538952 | tf_op jit(solution)/shard_map/ppermute | solution.py:208
  11.4 22.4 %collective-permute-start.1 = (f32[1,9,128,128]{3,2,1,0:T(8,128)S(1)}, f32[1,9,128,128]{3,2,1,0:T(8,128)S(1)}, u32[]{:S(2)}, u32[]{:S(2)}) collective-permute-start(f32[1,9,128,128]{3,2,1,0:T(8,128)S(1)} %slice_add_fusion.1), channel_id=1, source_target_pairs={{0,16},{8,24},{16,0},{24,8},{1,17},{9,25},{17,1},{25,9},{2,18},{10... | collective-permute-start | bytes 1769480 | tf_op jit(solution)/shard_map/ppermute | solution.py:208
  28.1 8.4 %collective-permute-start.5 = (f32[4,128,128]{2,1,0:T(8,128)S(1)}, f32[4,128,128]{2,1,0:T(8,128)S(1)}, u32[]{:S(2)}, u32[]{:S(2)}) collective-permute-start(f32[4,128,128]{2,1,0:T(8,128)S(1)} %pad_maximum_fusion.3), channel_id=1, source_target_pairs={{0,2},{1,3},{2,0},{3,1},{4,6},{5,7},{6,4},{7,5},{8,10},{9,11},{10,... | collective-permute-start | bytes 786440 | tf_op jit(solution)/shard_map/ppermute | solution.py:208
  28.2 8.4 %collective-permute-start.3 = (f32[4,128,128]{2,1,0:T(8,128)S(1)}, f32[4,128,128]{2,1,0:T(8,128)S(1)}, u32[]{:S(2)}, u32[]{:S(2)}) collective-permute-start(f32[4,128,128]{2,1,0:T(8,128)S(1)} %pad_maximum_fusion.2), channel_id=1, source_target_pairs={{0,1},{1,0},{2,3},{3,2},{4,5},{5,4},{6,7},{7,6},{8,9},{9,8},{10,11... | collective-permute-start | bytes 786440 | tf_op jit(solution)/shard_map/ppermute | solution.py:208
  34.0 9.4 %collective-permute-start.2 = (f32[2,7,128,128]{3,2,1,0:T(8,128)S(1)}, f32[2,7,128,128]{3,2,1,0:T(8,128)S(1)}, u32[]{:S(2)}, u32[]{:S(2)}) collective-permute-start(f32[2,7,128,128]{3,2,1,0:T(8,128)S(1)} %pad_maximum_fusion.1), channel_id=1, source_target_pairs={{0,8},{8,0},{16,24},{24,16},{1,9},{9,1},{17,25},{25,17},{2,10},{10... | collective-permute-start | bytes 2752520 | tf_op jit(solution)/shard_map/ppermute | solution.py:208
  36.6 5.0 %collective-permute-start.4 = (f32[2,128,128]{2,1,0:T(8,128)S(1)}, f32[2,128,128]{2,1,0:T(8,128)S(1)}, u32[]{:S(2)}, u32[]{:S(2)}) collective-permute-start(f32[2,128,128]{2,1,0:T(8,128)S(1)} %pad_maximum_fusion.4), channel_id=1, source_target_pairs={{0,2},{1,3},{2,0},{3,1},{4,6},{5,7},{6,4},{7,5},{8,10},{9,11},{10,... | collective-permute-start | bytes 393224 | tf_op jit(solution)/shard_map/ppermute | solution.py:208
  38.4 5.0 %collective-permute-start.6 = (f32[2,128,128]{2,1,0:T(8,128)S(1)}, f32[2,128,128]{2,1,0:T(8,128)S(1)}, u32[]{:S(2)}, u32[]{:S(2)}) collective-permute-start(f32[2,128,128]{2,1,0:T(8,128)S(1)} %pad_maximum_fusion.5), channel_id=1, source_target_pairs={{0,1},{1,0},{2,3},{3,2},{4,5},{5,4},{6,7},{7,6},{8,9},{9,8},{10,11... | collective-permute-start | bytes 393224 | tf_op jit(solution)/shard_map/ppermute | solution.py:208
  43.6 10.3 %collective-permute-start.8 = (f32[1,7,128,128]{3,2,1,0:T(8,128)S(1)}, f32[1,7,128,128]{3,2,1,0:T(8,128)S(1)}, u32[]{:S(2)}, u32[]{:S(2)}) collective-permute-start(f32[1,7,128,128]{3,2,1,0:T(8,128)S(1)} %get-tuple-element.25), channel_id=1, source_target_pairs={{0,16},{8,24},{16,0},{24,8},{1,17},{9,25},{17,1},{25,9},{2,18},{10... | collective-permute-start | bytes 1376264 | tf_op jit(solution)/shard_map/ppermute | solution.py:208
  44.0 7.3 %collective-permute-start.7 = (f32[2,128,128]{2,1,0:T(8,128)S(1)}, f32[2,128,128]{2,1,0:T(8,128)S(1)}, u32[]{:S(2)}, u32[]{:S(2)}) collective-permute-start(f32[2,128,128]{2,1,0:T(8,128)S(1)} %pad_maximum_fusion.6), channel_id=1, source_target_pairs={{0,4},{1,5},{2,6},{3,7},{4,0},{5,1},{6,2},{7,3},{8,12},{9,13},{10,... | collective-permute-start | bytes 393224 | tf_op jit(solution)/shard_map/ppermute | solution.py:208

commit v3 on v2

v3 whole, which is shorter than its diff:
```python
from functools import partial
import math

import jax
import jax.numpy as jnp
from jax import lax
from jax.experimental import pallas as pl
from jax.experimental.pallas import tpu as pltpu
from jax.sharding import PartitionSpec as P

BLK = 128
BLK_DEV = 8
PAIRS = BLK_DEV // 2
NONE = BLK_DEV
CORE = 1

NN = (((1,), (0,)), ((), ()))
NT = (((1,), (1,)), ((), ()))
TN = (((0,), (0,)), ((), ()))


def mm(a, b, dims):
    return lax.dot_general(a, b, dims, preferred_element_type=jnp.float32)


def list_items(lists, items, questions, base):
    first_block = lax.axis_index("ctx") * BLK_DEV
    below, above = first_block.astype(jnp.uint32), (first_block + BLK_DEV).astype(jnp.uint32)
    last = lists.shape[1] - 1
    end = base
    for i in questions:
        start = jnp.int32(0)
        stop = jnp.int32(0)
        for entry in range(last + 1):
            block = lists[i, entry].astype(jnp.uint32)
            start += (block < below).astype(jnp.int32)
            stop += (block < above).astype(jnp.int32)
        for p in range(PAIRS):
            at = start + 2 * p
            items[0, end + p] = i
            items[1, end + p] = lists[i, jnp.minimum(at, last)] - first_block
            items[2, end + p] = jnp.where(at + 1 < stop, lists[i, jnp.minimum(at + 1, last)] - first_block, NONE)
        end += (stop - start + 1) // 2
    for p in range(2):
        items[0, end + p] = questions[0]
        items[1, end + p] = NONE
        items[2, end + p] = NONE
    return end


def spread_lse(lse, out, rows):
    count, heads, tokens = lse.shape
    rest = lse[...].reshape(count * heads, tokens) * math.log2(math.e)
    row = lax.broadcasted_iota(jnp.int32, (tokens, rows), 1) // heads
    spread = (row == lax.broadcasted_iota(jnp.int32, (tokens, rows), 0)).astype(jnp.bfloat16)
    wide = jnp.zeros((count * heads, rows), jnp.float32)
    for _ in range(3):
        piece = rest.astype(jnp.bfloat16)
        rest = rest - piece.astype(jnp.float32)
        wide += mm(piece, spread, NN)
    head_of_row = lax.broadcasted_iota(jnp.int32, (heads, rows), 1) % heads
    own_head = head_of_row == lax.broadcasted_iota(jnp.int32, (heads, rows), 0)
    for i in range(count):
        picked = jnp.where(own_head, wide[i * heads : (i + 1) * heads], 0.0)
        out[i] = jnp.sum(picked, axis=0, keepdims=True)


def backward_kernel(
    factor,
    lists_hbm, lse_hbm, q_hbm, o_hbm, do_hbm, k_hbm, v_hbm,
    dq_ref, dk_ref, dv_ref,
    q_all, o_all, do_all, k_all, v_all, lse_all, delta_all, dk_acc, dv_acc,
    prob0, prob1, ds0, ds1, lse, lists, items, sems,
):
    prob_slots, ds_slots = (prob0, prob1), (ds0, ds1)
    count, rows, width = q_all.shape
    ctx_me, pb_me = lax.axis_index("ctx"), lax.axis_index("pb")
    copies = [
        pltpu.make_async_copy(src, dst, sems.at[n])
        for n, (src, dst) in enumerate(
            [(lists_hbm, lists), (lse_hbm, lse), (do_hbm, do_all), (o_hbm, o_all), (q_hbm, q_all)]
            + [(src, dst.at[pl.ds(0, BLK_DEV)]) for src, dst in ((k_hbm, k_all), (v_hbm, v_all))]
        )
    ]
    for copy in copies:
        copy.start()

    dq_ref[...] = jnp.zeros_like(dq_ref)
    dk_acc[...] = jnp.zeros_like(dk_acc)
    dv_acc[...] = jnp.zeros_like(dv_acc)
    k_all[NONE] = jnp.zeros((BLK, width), k_all.dtype)
    v_all[NONE] = jnp.zeros((BLK, width), v_all.dtype)
    copies[0].wait()
    total = list_items(lists, items, range(count), jnp.int32(0))
    copies[1].wait()
    spread_lse(lse, lse_all, rows)
    scale = factor * math.log2(math.e)
    parts, part_rows = dq_ref.shape[0], dq_ref.shape[2]

    def row_deltas(questions):
        ones = jnp.ones((8, 2 * width), jnp.bfloat16)
        for i in questions:
            product = do_all[i].astype(jnp.float32) * o_all[i].astype(jnp.float32)
            high = product.astype(jnp.bfloat16)
            low = (product - high.astype(jnp.float32)).astype(jnp.bfloat16)
            delta_all[i] = mm(ones, jnp.concatenate([high, low], axis=1), NT)[0:1]

    def scores(item, slot):
        i, b0, b1 = items[0, item], items[1, item], items[2, item]
        keys = jnp.concatenate([k_all[b0], k_all[b1]], axis=0)
        values = jnp.concatenate([v_all[b0], v_all[b1]], axis=0)
        prob = jnp.exp2(mm(keys, q_all[i], NT) * scale - lse_all[i])
        dprob = mm(values, do_all[i], NT)
        prob_slots[slot][...] = prob.astype(jnp.bfloat16)
        ds_slots[slot][...] = (prob * (dprob - delta_all[i])).astype(jnp.bfloat16)

    def gradients(item, slot):
        i, b0, b1 = items[0, item], items[1, item], items[2, item]
        keys = jnp.concatenate([k_all[b0], k_all[b1]], axis=0)
        dscore = ds_slots[slot][...]
        dv = mm(prob_slots[slot][...], do_all[i], NN)
        dk = mm(dscore, q_all[i], NN)
        dq = mm(dscore, keys, TN) * factor
        for j in range(parts):
            dq_ref[ctx_me ^ j, i] += dq[j * part_rows : (j + 1) * part_rows]
        dv_acc[b0] += dv[:BLK]
        dk_acc[b0] += dk[:BLK]
        dv_acc[b1] += dv[BLK:]
        dk_acc[b1] += dk[BLK:]

    def sweep(base, total):
        def several(first, step_items):
            def body(step, carry):
                at = first + step_items * step
                for n in range(0, step_items, 2):
                    scores(at + n + 1, 1)
                    gradients(at + n, 0)
                    scores(at + n + 2, 0)
                    gradients(at + n + 1, 1)
                return carry

            return body

        scores(base, 0)
        eights = total // 8
        lax.fori_loop(0, eights, several(base, 8), 0)
        lax.fori_loop(0, (total - 8 * eights + 1) // 2, several(base + 8 * eights, 2), 0)

    for copy in copies[2:]:
        copy.wait()
    row_deltas(range(count))
    sweep(jnp.int32(0), total)

    parts, part_rows = dk_ref.shape[0], dk_ref.shape[1]
    per = BLK // part_rows
    for j in range(parts):
        dest = pb_me ^ j
        at = pl.multiple_of((dest % per) * part_rows, part_rows)
        dk_ref[j] = dk_acc[dest // per, pl.ds(at, part_rows)] * factor
        dv_ref[j] = dv_acc[dest // per, pl.ds(at, part_rows)]


def backward(lists, lse, queries, outputs, grads, keys, values, sizes):
    ctx_size, pb_size = sizes
    count, rows, width = queries.shape
    grad = pltpu.VMEM((pb_size, BLK_DEV * BLK // pb_size, width), jnp.float32)
    f32, bf16 = jnp.float32, jnp.bfloat16
    own_rows = pltpu.VMEM((count, rows, width), bf16)
    block = pltpu.VMEM((BLK_DEV + 1, BLK, width), bf16)
    row = pltpu.VMEM((count, 1, rows), f32)
    acc = pltpu.VMEM((BLK_DEV + 1, BLK, width), f32)
    slot = pltpu.VMEM((2 * BLK, rows), bf16)
    in_hbm = [pltpu.with_memory_space_constraint(a, pltpu.HBM) for a in (lists, lse, queries, outputs, grads, keys, values)]
    return pl.pallas_call(
        partial(backward_kernel, width ** (-0.5)),
        in_specs=[pl.BlockSpec(memory_space=pltpu.HBM)] * 7,
        out_specs=[pl.BlockSpec(memory_space=pltpu.VMEM)] * 3,
        out_shape=[pltpu.VMEM((ctx_size, count, rows // ctx_size, width), f32), grad, grad],
        scratch_shapes=[own_rows] * 3
        + [block, block, row, row, acc, acc]
        + [slot] * 4
        + [
            pltpu.VMEM(lse.shape, f32),
            pltpu.SMEM(lists.shape, jnp.int32),
            pltpu.SMEM((3, (count + 1) * PAIRS), jnp.int32),
            pltpu.SemaphoreType.DMA((7,)),
        ],
        compiler_params=pltpu.CompilerParams(vmem_limit_bytes=24 * 1024 * 1024),
        cost_estimate=pl.CostEstimate(
            flops=count * rows * BLK_DEV * BLK * width * 10, bytes_accessed=count * rows * width * 12, transcendentals=0
        ),
        name="attention_backward",
    )(*in_hbm)


def swap(array, axis, size, bit):
    return lax.ppermute(array, axis, [(i, i ^ bit) for i in range(size)])


def exchange(groups, axis, size, bit):
    sent = jnp.stack([parts[j] for parts in groups for j in sorted(parts) if j & bit])
    got = iter(swap(sent, axis, size, bit))
    return [{j: parts[j] + next(got) for j in sorted(parts) if not j & bit} for parts in groups]


def bits_of(size):
    return [1 << i for i in range(size.bit_length() - 1)]


def sum_two_ways(first, second, axis, size):
    order = bits_of(size)
    other = order[1::-1] + order[2:]
    for one, two in zip(order, other):
        if one == two:
            first, second = exchange([first, second], axis, size, one)
        else:
            (first,) = exchange([first], axis, size, one)
            (second,) = exchange([second], axis, size, two)
    return first[0], second[0]


def in_one_piece(function, *operands):
    shapes = jax.eval_shape(function, *operands)
    zeros = lambda *_: jax.tree.map(lambda s: jnp.zeros(s.shape, s.dtype), shapes)
    return lax.cond(lax.optimization_barrier(jnp.int32(1)) > 0, function, zeros, *operands)


def local(ctx_size, pb_size, queries, keys, values, outputs_saved, grad_out, saved_lse, block_lists):
    questions, tokens, heads, width = queries.shape
    rows = tokens * heads
    flat = lambda a: a.reshape(questions, rows, width)
    blocked = lambda a: a.reshape(BLK_DEV, BLK, width)
    dq, dk, dv = backward(
        block_lists,
        jnp.swapaxes(saved_lse, 1, 2),
        flat(queries),
        flat(outputs_saved),
        flat(grad_out),
        blocked(keys),
        blocked(values),
        (ctx_size, pb_size),
    )
    far = [j for j in range(2, ctx_size, 2)]
    got = swap(jnp.stack([dq[j | CORE] for j in far]), "ctx", ctx_size, CORE)
    parts = {j: dq[j] + got[n] for n, j in enumerate(far)}
    own, near, dk, dv, parts = lax.optimization_barrier((dq[0], dq[CORE], dk, dv, parts))
    arrived = []
    for bit in bits_of(ctx_size)[1:]:
        sent = [j for j in sorted(parts) if j & bit]
        got = dict(zip(sent, swap(jnp.stack([parts[j] for j in sent]), "ctx", ctx_size, bit)))
        arrived.append(got.pop(bit))
        parts = {j: parts[j] + got[j | bit] for j in parts if not j & bit}
    own = lax.optimization_barrier(own + swap(near, "ctx", ctx_size, CORE))
    by_dest = lambda a: {j: a[j] for j in range(pb_size)}
    sums = partial(sum_two_ways, axis="pb", size=pb_size)
    key_grad, value_grad = in_one_piece(sums, by_dest(dk), by_dest(dv))
    query_grad = sum(arrived, own)
    return query_grad.reshape(questions, tokens // ctx_size, heads, width), key_grad, value_grad


def solution(mesh):
    ctx_size, pb_size = mesh.shape["ctx"], mesh.shape["pb"]
    placed = (
        P("pb", None, None, None),
        P("ctx", None),
        P("ctx", None),
        P("pb", None, None, None),
        P("pb", None, None, None),
        P("pb", None, None),
        P("pb", None),
    )
    return jax.shard_map(
        partial(local, ctx_size, pb_size),
        mesh=mesh,
        in_specs=placed,
        out_specs=(P("pb", "ctx", None, None), P(("ctx", "pb"), None), P(("ctx", "pb"), None)),
        check_vma=False,
    )
```

time: 55.7 us -> 53.8 us (0.966)
  waiting for transfers between devices: 20.6 us -> 17.7 us
  other arithmetic: 2.32 us -> 5.16 us
  starting transfers between devices: 15.5 us -> 13.5 us
    ppermute x9 -> x8, waiting for transfers between devices: 20.6 us -> 17.7 us  [swap(): return lax.ppermute(array, axis, [(i, i ^ bit) for i in range(size)])]
    add x0 -> x2, other arithmetic: none -> 2.67 us  [the longest x1 1.37 us: local(): own = lax.optimization_barrier(own + swap(near, 'ctx', ctx_size, CORE))]
    ppermute x9 -> x8, starting transfers between devices: 15.5 us -> 13.5 us  [swap(): return lax.ppermute(array, axis, [(i, i ^ bit) for i in range(size)])]
    reshape x1, other arithmetic: 1.04 us -> 2.31 us  [local(): query_grad.reshape(questions, tokens // ctx_size, heads, width)]
    add x8 -> x4, other arithmetic: 1.05 us -> 0.11 us  [exchange(): parts[j] + next(got)]
    pallas_call x2 -> x1, Pallas kernels: 15.6 us -> 15.8 us  [backward(): pl.pallas_call(partial(backward_kernel, width ** (-0.5)), in_specs=[pl.Bl...]
  transfers between devices with their start and end apart: 9 -> 8, of which waited for: 8 -> 6; matrix products, arithmetic and copies ran while one was open for 2% -> 3% of each run, Pallas kernels for 15% -> 0%
where the time goes in v3:
time: 53.8 us; the launch traced here: 53 us
  waiting for transfers between devices  17.7 us (33%)
  Pallas kernels  15.8 us (29%)
  starting transfers between devices  13.5 us (25%)
  other arithmetic  5.16 us (10%)
  between operations  0.69 us (1%)
    ppermute x8, waiting for transfers between devices, swap(): return lax.ppermute(array, axis, [(i, i ^ bit) for i in range(size)])  17.7 us
    pallas_call x1, Pallas kernels, backward(): pl.pallas_call(partial(backward_kernel, width ** (-0.5)), in_specs=[pl.Bl...  15.8 us
    ppermute x8, starting transfers between devices, swap(): return lax.ppermute(array, axis, [(i, i ^ bit) for i in range(size)])  13.5 us
    reshape x1, other arithmetic, local(): query_grad.reshape(questions, tokens // ctx_size, heads, width)  2.31 us
    add x1, other arithmetic, local(): own = lax.optimization_barrier(own + swap(near, 'ctx', ctx_size, CORE))  1.37 us
    add x1, other arithmetic, local(): parts = {j: dq[j] + got[n] for n, j in enumerate(far)}  1.3 us
  transfers between devices with their start and end apart: 8, of which 6 were waited for; matrix products, arithmetic and copies ran while one was open for 3% of the time, Pallas kernels for 0%

profile of v3, /device:TPU:0, one launch (start us, length us, event | category | flops | bytes accessed | tf_op | source)
XLA Modules:
  0.0 53.0 jit_solution(4815421665408449559)
XLA Ops:
  0.6 15.8 %attention_backward.1 = (f32[4,16,128,128]{3,2,1,0:T(8,128)S(1)}, f32[8,128,128]{2,1,0:T(8,128)S(1)}, f32[8,128,128]{2,1,0:T(8,128)S(1)}) custom-call(s32[16,24]{1,0:T(8,128)} %lists_hbm.1, f32[16,8,64]{2,1,0:T(8,128)} %bitcast.29, bf16[16,512,128]{2,1,0:T(8,128)(2,1)} %bitcast.24, bf16[16,512,128]{2,1,0:T(8,128)(2,1)} %bitcast.25, ...), custom_call_target="tpu_custom_call" | custom-call | flops 10737418240 | bytes 12582912 | tf_op jit(solution)/shard_map/attention_backward/pallas_call | solution.py:174
  16.4 0.1 slice.79
  16.5 1.4 %collective-permute-start.5 = (f32[1,16,128,128]{3,2,1,0:T(8,128)S(1)}, f32[1,16,128,128]{3,2,1,0:T(8,128)S(1)}, u32[]{:S(2)}, u32[]{:S(2)}) collective-permute-start(f32[1,16,128,128]{3,2,1,0:T(8,128)S(1)} %slice.79), channel_id=1, source_target_pairs={{0,8},{8,0},{16,24},{24,16},{1,9},{9,1},{17,25},{25,17},{2,10},{10... | collective-permute-start | bytes 3145736 | tf_op jit(solution)/shard_map/ppermute | solution.py:197
  17.9 2.3 %collective-permute-done.5 = f32[1,16,128,128]{3,2,1,0:T(8,128)S(1)} collective-permute-done((f32[1,16,128,128]{3,2,1,0:T(8,128)S(1)}, f32[1,16,128,128]{3,2,1,0:T(8,128)S(1)}, u32[]{:S(2)}, u32[]{:S(2)}) %collective-permute-start.5) | collective-permute-done | bytes 1048608 | tf_op jit(solution)/shard_map/ppermute | solution.py:197
  20.2 1.3 %add_bitcast_fusion = (f32[16,128,128]{2,1,0:T(8,128)S(1)}, f32[16,128,128]{2,1,0:T(8,128)}, f32[16,128,128]{2,1,0:T(8,128)S(1)}) fusion(f32[1,16,128,128]{3,2,1,0:T(8,128)S(1)} %collective-permute-done.5, f32[4,16,128,128]{3,2,1,0:T(8,128)S(1)} %get-tuple-element.57), kind=kLoop, calls=%fused_computation.23 | loop fusion | flops 262144 | bytes 7340032 | tf_op jit(solution)/shard_map/add | solution.py:245
  21.5 0.4 collective-permute-start.6
  21.9 2.1 %collective-permute-start.7 = (f32[1,16,128,128]{3,2,1,0:T(8,128)S(1)}, f32[1,16,128,128]{3,2,1,0:T(8,128)}, u32[]{:S(2)}, u32[]{:S(2)}) collective-permute-start(f32[1,16,128,128]{3,2,1,0:T(8,128)S(1)} %bitcast.23), channel_id=1, source_target_pairs={{0,16},{8,24},{16,0},{24,8},{1,17},{9,25},{17,1},{25,9},{2,18},{10... | collective-permute-start | bytes 3145736 | tf_op jit(solution)/shard_map/ppermute | solution.py:197
  24.0 25.3 %conditional.1 = (f32[128,128]{1,0:T(8,128)S(1)}, f32[128,128]{1,0:T(8,128)S(1)}) conditional(s32[]{:T(128)} %convert_element_type.3, () %tuple.18, (f32[8,128,128]{2,1,0:T(8,128)S(1)}, f32[8,128,128]{2,1,0:T(8,128)S(1)}) %tuple.19), branch_computations={%region_0.0_spmd, %region_1.0_spmd} | conditional | flops 589824 | bytes 8519896 | solution.py:225
  24.0 2.6 %collective-permute-start = (f32[4,128,128]{2,1,0:T(8,128)S(1)}, f32[4,128,128]{2,1,0:T(8,128)S(1)}, u32[]{:S(2)}, u32[]{:S(2)}) collective-permute-start(f32[4,128,128]{2,1,0:T(8,128)S(1)} %pad_maximum_fusion), channel_id=1, source_target_pairs={{0,1},{1,0},{2,3},{3,2},{4,5},{5,4},{6,7},{7,6},{8,9},{9,8},{10,11... | collective-permute-start | bytes 786440 | tf_op jit(solution)/shard_map/cond/branch_1_fun/ppermute | solution.py:197
  26.7 2.0 %collective-permute-start.2 = (f32[4,128,128]{2,1,0:T(8,128)S(1)}, f32[4,128,128]{2,1,0:T(8,128)S(1)}, u32[]{:S(2)}, u32[]{:S(2)}) collective-permute-start(f32[4,128,128]{2,1,0:T(8,128)S(1)} %pad_maximum_fusion.1), channel_id=1, source_target_pairs={{0,2},{1,3},{2,0},{3,1},{4,6},{5,7},{6,4},{7,5},{8,10},{9,11},{10,... | collective-permute-start | bytes 786440 | tf_op jit(solution)/shard_map/cond/branch_1_fun/ppermute | solution.py:197
  28.7 4.8 %collective-permute-done = f32[4,128,128]{2,1,0:T(8,128)S(1)} collective-permute-done((f32[4,128,128]{2,1,0:T(8,128)S(1)}, f32[4,128,128]{2,1,0:T(8,128)S(1)}, u32[]{:S(2)}, u32[]{:S(2)}) %collective-permute-start) | collective-permute-done | bytes 262176 | tf_op jit(solution)/shard_map/cond/branch_1_fun/ppermute | solution.py:197
  33.5 1.6 %collective-permute-done.2 = f32[4,128,128]{2,1,0:T(8,128)S(1)} collective-permute-done((f32[4,128,128]{2,1,0:T(8,128)S(1)}, f32[4,128,128]{2,1,0:T(8,128)S(1)}, u32[]{:S(2)}, u32[]{:S(2)}) %collective-permute-start.2) | collective-permute-done | bytes 262176 | tf_op jit(solution)/shard_map/cond/branch_1_fun/ppermute | solution.py:197
  35.1 1.5 %collective-permute-start.1 = (f32[2,128,128]{2,1,0:T(8,128)S(1)}, f32[2,128,128]{2,1,0:T(8,128)S(1)}, u32[]{:S(2)}, u32[]{:S(2)}) collective-permute-start(f32[2,128,128]{2,1,0:T(8,128)S(1)} %pad_maximum_fusion.2), channel_id=1, source_target_pairs={{0,2},{1,3},{2,0},{3,1},{4,6},{5,7},{6,4},{7,5},{8,10},{9,11},{10,... | collective-permute-start | bytes 393224 | tf_op jit(solution)/shard_map/cond/branch_1_fun/ppermute | solution.py:197
  36.6 0.4 collective-permute-start.3
  37.0 3.2 %collective-permute-done.1 = f32[2,128,128]{2,1,0:T(8,128)S(1)} collective-permute-done((f32[2,128,128]{2,1,0:T(8,128)S(1)}, f32[2,128,128]{2,1,0:T(8,128)S(1)}, u32[]{:S(2)}, u32[]{:S(2)}) %collective-permute-start.1) | collective-permute-done | bytes 131104 | tf_op jit(solution)/shard_map/cond/branch_1_fun/ppermute | solution.py:197
  40.2 1.5 %collective-permute-done.3 = f32[2,128,128]{2,1,0:T(8,128)S(1)} collective-permute-done((f32[2,128,128]{2,1,0:T(8,128)S(1)}, f32[2,128,128]{2,1,0:T(8,128)S(1)}, u32[]{:S(2)}, u32[]{:S(2)}) %collective-permute-start.3) | collective-permute-done | bytes 131104 | tf_op jit(solution)/shard_map/cond/branch_1_fun/ppermute | solution.py:197
  41.7 3.2 %collective-permute-start.4 = (f32[2,128,128]{2,1,0:T(8,128)S(1)}, f32[2,128,128]{2,1,0:T(8,128)S(1)}, u32[]{:S(2)}, u32[]{:S(2)}) collective-permute-start(f32[2,128,128]{2,1,0:T(8,128)S(1)} %pad_maximum_fusion.4), channel_id=1, source_target_pairs={{0,4},{1,5},{2,6},{3,7},{4,0},{5,1},{6,2},{7,3},{8,12},{9,13},{10,... | collective-permute-start | bytes 393224 | tf_op jit(solution)/shard_map/cond/branch_1_fun/ppermute | solution.py:197
  44.9 4.3 %collective-permute-done.4 = f32[2,128,128]{2,1,0:T(8,128)S(1)} collective-permute-done((f32[2,128,128]{2,1,0:T(8,128)S(1)}, f32[2,128,128]{2,1,0:T(8,128)S(1)}, u32[]{:S(2)}, u32[]{:S(2)}) %collective-permute-start.4) | collective-permute-done | bytes 131104 | tf_op jit(solution)/shard_map/cond/branch_1_fun/ppermute | solution.py:197
  49.3 0.0 copy-start
  49.3 0.0 copy-start.1
  49.3 0.0 collective-permute-done.6
  49.3 1.4 %add.74 = f32[16,128,128]{2,1,0:T(8,128)S(1)} add(f32[16,128,128]{2,1,0:T(8,128)S(1)} %get-tuple-element.60, f32[16,128,128]{2,1,0:T(8,128)} %collective-permute-done.6) | non-fusion elementwise | flops 262144 | bytes 3145728 | tf_op jit(solution)/shard_map/add | solution.py:253
  50.7 0.0 collective-permute-done.7
  50.7 2.3 %fusion.2 = f32[16,16,8,128]{3,2,1,0:T(8,128)} fusion(f32[16,128,128]{2,1,0:T(8,128)S(1)} %add.74, f32[1,16,128,128]{3,2,1,0:T(8,128)} %collective-permute-done.7), kind=kLoop, calls=%fused_computation.22 | loop fusion | flops 262144 | bytes 3145728 | tf_op jit(solution)/shard_map/reshape | solution.py:258
  53.0 0.0 copy-done
  53.0 0.0 copy-done.1
  (11 shorter events, 0.2 us)
Async XLA Ops:
  16.5 3.7 %collective-permute-start.5 = (f32[1,16,128,128]{3,2,1,0:T(8,128)S(1)}, f32[1,16,128,128]{3,2,1,0:T(8,128)S(1)}, u32[]{:S(2)}, u32[]{:S(2)}) collective-permute-start(f32[1,16,128,128]{3,2,1,0:T(8,128)S(1)} %slice.79), channel_id=1, source_target_pairs={{0,8},{8,0},{16,24},{24,16},{1,9},{9,1},{17,25},{25,17},{2,10},{10... | collective-permute-start | bytes 3145736 | tf_op jit(solution)/shard_map/ppermute | solution.py:197
  21.5 27.8 %collective-permute-start.6 = (f32[16,128,128]{2,1,0:T(8,128)}, f32[16,128,128]{2,1,0:T(8,128)}, u32[]{:S(2)}, u32[]{:S(2)}) collective-permute-start(f32[16,128,128]{2,1,0:T(8,128)} %get-tuple-element.61), channel_id=1, source_target_pairs={{0,8},{8,0},{16,24},{24,16},{1,9},{9,1},{17,25},{25,17},{2,10},{10... | collective-permute-start | bytes 3145736 | tf_op jit(solution)/shard_map/ppermute | solution.py:197
  21.9 28.8 %collective-permute-start.7 = (f32[1,16,128,128]{3,2,1,0:T(8,128)S(1)}, f32[1,16,128,128]{3,2,1,0:T(8,128)}, u32[]{:S(2)}, u32[]{:S(2)}) collective-permute-start(f32[1,16,128,128]{3,2,1,0:T(8,128)S(1)} %bitcast.23), channel_id=1, source_target_pairs={{0,16},{8,24},{16,0},{24,8},{1,17},{9,25},{17,1},{25,9},{2,18},{10... | collective-permute-start | bytes 3145736 | tf_op jit(solution)/shard_map/ppermute | solution.py:197
  24.0 9.4 %collective-permute-start = (f32[4,128,128]{2,1,0:T(8,128)S(1)}, f32[4,128,128]{2,1,0:T(8,128)S(1)}, u32[]{:S(2)}, u32[]{:S(2)}) collective-permute-start(f32[4,128,128]{2,1,0:T(8,128)S(1)} %pad_maximum_fusion), channel_id=1, source_target_pairs={{0,1},{1,0},{2,3},{3,2},{4,5},{5,4},{6,7},{7,6},{8,9},{9,8},{10,11... | collective-permute-start | bytes 786440 | tf_op jit(solution)/shard_map/cond/branch_1_fun/ppermute | solution.py:197
  26.7 8.4 %collective-permute-start.2 = (f32[4,128,128]{2,1,0:T(8,128)S(1)}, f32[4,128,128]{2,1,0:T(8,128)S(1)}, u32[]{:S(2)}, u32[]{:S(2)}) collective-permute-start(f32[4,128,128]{2,1,0:T(8,128)S(1)} %pad_maximum_fusion.1), channel_id=1, source_target_pairs={{0,2},{1,3},{2,0},{3,1},{4,6},{5,7},{6,4},{7,5},{8,10},{9,11},{10,... | collective-permute-start | bytes 786440 | tf_op jit(solution)/shard_map/cond/branch_1_fun/ppermute | solution.py:197
  35.1 5.0 %collective-permute-start.1 = (f32[2,128,128]{2,1,0:T(8,128)S(1)}, f32[2,128,128]{2,1,0:T(8,128)S(1)}, u32[]{:S(2)}, u32[]{:S(2)}) collective-permute-start(f32[2,128,128]{2,1,0:T(8,128)S(1)} %pad_maximum_fusion.2), channel_id=1, source_target_pairs={{0,2},{1,3},{2,0},{3,1},{4,6},{5,7},{6,4},{7,5},{8,10},{9,11},{10,... | collective-permute-start | bytes 393224 | tf_op jit(solution)/shard_map/cond/branch_1_fun/ppermute | solution.py:197
  36.6 5.0 %collective-permute-start.3 = (f32[2,128,128]{2,1,0:T(8,128)S(1)}, f32[2,128,128]{2,1,0:T(8,128)S(1)}, u32[]{:S(2)}, u32[]{:S(2)}) collective-permute-start(f32[2,128,128]{2,1,0:T(8,128)S(1)} %pad_maximum_fusion.3), channel_id=1, source_target_pairs={{0,1},{1,0},{2,3},{3,2},{4,5},{5,4},{6,7},{7,6},{8,9},{9,8},{10,11... | collective-permute-start | bytes 393224 | tf_op jit(solution)/shard_map/cond/branch_1_fun/ppermute | solution.py:197
  41.7 7.5 %collective-permute-start.4 = (f32[2,128,128]{2,1,0:T(8,128)S(1)}, f32[2,128,128]{2,1,0:T(8,128)S(1)}, u32[]{:S(2)}, u32[]{:S(2)}) collective-permute-start(f32[2,128,128]{2,1,0:T(8,128)S(1)} %pad_maximum_fusion.4), channel_id=1, source_target_pairs={{0,4},{1,5},{2,6},{3,7},{4,0},{5,1},{6,2},{7,3},{8,12},{9,13},{10,... | collective-permute-start | bytes 393224 | tf_op jit(solution)/shard_map/cond/branch_1_fun/ppermute | solution.py:197
  49.3 3.7 %copy-start = (f32[128,128]{1,0:T(8,128)}, f32[128,128]{1,0:T(8,128)S(1)}, u32[]{:S(2)}) copy-start(f32[128,128]{1,0:T(8,128)S(1)} %get-tuple-element.55) | copy-start | bytes 196612
  49.3 3.7 %copy-start.1 = (f32[128,128]{1,0:T(8,128)}, f32[128,128]{1,0:T(8,128)S(1)}, u32[]{:S(2)}) copy-start(f32[128,128]{1,0:T(8,128)S(1)} %get-tuple-element.56) | copy-start | bytes 196612

commit v4 on v3

--- a/solution.py
+++ b/solution.py
@@ -193,6 +193,43 @@
     )(*in_hbm)
 
 
+def sum_kernel(cuts, *refs):
+    ins, out, slots, sems = refs[: len(refs) // 2 - 1], refs[len(refs) // 2 - 1], refs[len(refs) // 2 : -1], refs[-1]
+    rows = out.shape[0] // cuts
+    cut = lambda ref, n: ref.at[pl.ds(n * rows, rows)]
+    loads = [
+        [pltpu.make_async_copy(cut(src, n), cut(dst, n), sems.at[m, n]) for m, (src, dst) in enumerate(zip(ins, slots))]
+        for n in range(cuts)
+    ]
+    stores = [pltpu.make_async_copy(cut(slots[-1], n), cut(out, n), sems.at[len(ins), n]) for n in range(cuts)]
+    for load in loads:
+        for copy in load:
+            copy.start()
+    for n, load in enumerate(loads):
+        for copy in load:
+            copy.wait()
+        total = cut(slots[0], n)[...]
+        for slot in slots[1:-1]:
+            total += cut(slot, n)[...]
+        cut(slots[-1], n)[...] = total
+        stores[n].start()
+    for store in stores:
+        store.wait()
+
+
+def sum_in_hbm(arrays, cuts=4):
+    like, n = arrays[0], len(arrays)
+    return pl.pallas_call(
+        partial(sum_kernel, cuts),
+        in_specs=[pl.BlockSpec(memory_space=pl.ANY)] * n,
+        out_specs=pl.BlockSpec(memory_space=pltpu.HBM),
+        out_shape=pltpu.HBM(like.shape, like.dtype),
+        scratch_shapes=[pltpu.VMEM(like.shape, like.dtype)] * (n + 1) + [pltpu.SemaphoreType.DMA((n + 1, cuts))],
+        compiler_params=pltpu.CompilerParams(vmem_limit_bytes=12 * 1024 * 1024),
+        name="sum_parts",
+    )(*arrays)
+
+
 def swap(array, axis, size, bit):
     return lax.ppermute(array, axis, [(i, i ^ bit) for i in range(size)])
 
@@ -254,7 +291,7 @@
     by_dest = lambda a: {j: a[j] for j in range(pb_size)}
     sums = partial(sum_two_ways, axis="pb", size=pb_size)
     key_grad, value_grad = in_one_piece(sums, by_dest(dk), by_dest(dv))
-    query_grad = sum(arrived, own)
+    query_grad = sum_in_hbm([own] + arrived)
     return query_grad.reshape(questions, tokens // ctx_size, heads, width), key_grad, value_grad
 
 

time: 53.8 us -> 52.9 us (0.983)
  other arithmetic: 5.16 us -> 3.23 us
  starting transfers between devices: 13.5 us -> 15.4 us
  waiting for transfers between devices: 17.7 us -> 16.5 us
    reshape x1 -> x0, other arithmetic: 2.31 us -> none  [local(): query_grad.reshape(questions, tokens // ctx_size, heads, width)]
    ppermute x8, starting transfers between devices: 13.5 us -> 15.4 us  [swap(): return lax.ppermute(array, axis, [(i, i ^ bit) for i in range(size)])]
    pallas_call x0 -> x1, Pallas kernels: none -> 1.25 us  [sum_in_hbm(): pl.pallas_call(partial(sum_kernel, cuts), in_specs=[pl.BlockSpec(memory_s...]
    ppermute x8, waiting for transfers between devices: 17.7 us -> 16.5 us  [swap(): return lax.ppermute(array, axis, [(i, i ^ bit) for i in range(size)])]
    pallas_call x1, Pallas kernels: 15.8 us -> 14.9 us  [backward(): pl.pallas_call(partial(backward_kernel, width ** (-0.5)), in_specs=[pl.Bl...]
where the time goes in v4:
time: 52.9 us; the launch traced here: 52.2 us
  waiting for transfers between devices  16.5 us (31%)
  Pallas kernels  16.2 us (31%)
  starting transfers between devices  15.4 us (29%)
  other arithmetic  3.23 us (6%)
  between operations  0.7 us (1%)
    ppermute x8, waiting for transfers between devices, swap(): return lax.ppermute(array, axis, [(i, i ^ bit) for i in range(size)])  16.5 us
    ppermute x8, starting transfers between devices, swap(): return lax.ppermute(array, axis, [(i, i ^ bit) for i in range(size)])  15.4 us
    pallas_call x1, Pallas kernels, backward(): pl.pallas_call(partial(backward_kernel, width ** (-0.5)), in_specs=[pl.Bl...  14.9 us
    add x1, other arithmetic, local(): parts = {j: dq[j] + got[n] for n, j in enumerate(far)}  1.68 us
    add x1, other arithmetic, local(): own = lax.optimization_barrier(own + swap(near, 'ctx', ctx_size, CORE))  1.37 us
    pallas_call x1, Pallas kernels, sum_in_hbm(): pl.pallas_call(partial(sum_kernel, cuts), in_specs=[pl.BlockSpec(memory_s...  1.25 us
  transfers between devices with their start and end apart: 8, of which 6 were waited for; matrix products, arithmetic and copies ran while one was open for 3% of the time, Pallas kernels for 0%

profile of v4, /device:TPU:0, one launch (start us, length us, event | category | flops | bytes accessed | tf_op | source)
XLA Modules:
  0.0 52.2 jit_solution(944382617670973877)
XLA Ops:
  0.6 14.9 %attention_backward.1 = (f32[4,16,128,128]{3,2,1,0:T(8,128)S(1)}, f32[8,128,128]{2,1,0:T(8,128)S(1)}, f32[8,128,128]{2,1,0:T(8,128)S(1)}) custom-call(s32[16,24]{1,0:T(8,128)} %lists_hbm.1, f32[16,8,64]{2,1,0:T(8,128)} %bitcast.26, bf16[16,512,128]{2,1,0:T(8,128)(2,1)} %bitcast.21, bf16[16,512,128]{2,1,0:T(8,128)(2,1)} %bitcast.22, ...), custom_call_target="tpu_custom_call" | custom-call | flops 10737418240 | bytes 12582912 | tf_op jit(solution)/shard_map/attention_backward/pallas_call | solution.py:174
  15.6 0.1 slice.79
  15.7 1.4 %collective-permute-start.5 = (f32[1,16,128,128]{3,2,1,0:T(8,128)S(1)}, f32[1,16,128,128]{3,2,1,0:T(8,128)S(1)}, u32[]{:S(2)}, u32[]{:S(2)}) collective-permute-start(f32[1,16,128,128]{3,2,1,0:T(8,128)S(1)} %slice.79), channel_id=1, source_target_pairs={{0,8},{8,0},{16,24},{24,16},{1,9},{9,1},{17,25},{25,17},{2,10},{10... | collective-permute-start | bytes 3145736 | tf_op jit(solution)/shard_map/ppermute | solution.py:234
  17.0 2.3 %collective-permute-done.5 = f32[1,16,128,128]{3,2,1,0:T(8,128)S(1)} collective-permute-done((f32[1,16,128,128]{3,2,1,0:T(8,128)S(1)}, f32[1,16,128,128]{3,2,1,0:T(8,128)S(1)}, u32[]{:S(2)}, u32[]{:S(2)}) %collective-permute-start.5) | collective-permute-done | bytes 1048608 | tf_op jit(solution)/shard_map/ppermute | solution.py:234
  19.3 1.7 %add_bitcast_fusion = (f32[16,128,128]{2,1,0:T(8,128)}, f32[16,128,128]{2,1,0:T(8,128)}, f32[16,128,128]{2,1,0:T(8,128)S(1)}) fusion(f32[1,16,128,128]{3,2,1,0:T(8,128)S(1)} %collective-permute-done.5, f32[4,16,128,128]{3,2,1,0:T(8,128)S(1)} %get-tuple-element.57), kind=kLoop, calls=%fused_computation.21 | loop fusion | flops 262144 | bytes 7340032 | tf_op jit(solution)/shard_map/add | solution.py:282
  21.0 0.4 collective-permute-start.6
  21.4 3.0 %collective-permute-start.7 = (f32[1,16,128,128]{3,2,1,0:T(8,128)}, f32[1,16,128,128]{3,2,1,0:T(8,128)S(1)}, u32[]{:S(2)}, u32[]{:S(2)}) collective-permute-start(f32[1,16,128,128]{3,2,1,0:T(8,128)} %bitcast.11), channel_id=1, source_target_pairs={{0,16},{8,24},{16,0},{24,8},{1,17},{9,25},{17,1},{25,9},{2,18},{10... | collective-permute-start | bytes 3145736 | tf_op jit(solution)/shard_map/ppermute | solution.py:234
  24.4 25.2 %conditional.1 = (f32[128,128]{1,0:T(8,128)S(1)}, f32[128,128]{1,0:T(8,128)S(1)}) conditional(s32[]{:T(128)} %convert_element_type.3, () %tuple.18, (f32[8,128,128]{2,1,0:T(8,128)S(1)}, f32[8,128,128]{2,1,0:T(8,128)S(1)}) %tuple.19), branch_computations={%region_0.0_spmd, %region_1.0_spmd} | conditional | flops 589824 | bytes 8519896 | solution.py:262
  24.4 1.6 %collective-permute-start = (f32[4,128,128]{2,1,0:T(8,128)S(1)}, f32[4,128,128]{2,1,0:T(8,128)S(1)}, u32[]{:S(2)}, u32[]{:S(2)}) collective-permute-start(f32[4,128,128]{2,1,0:T(8,128)S(1)} %pad_maximum_fusion), channel_id=1, source_target_pairs={{0,1},{1,0},{2,3},{3,2},{4,5},{5,4},{6,7},{7,6},{8,9},{9,8},{10,11... | collective-permute-start | bytes 786440 | tf_op jit(solution)/shard_map/cond/branch_1_fun/ppermute | solution.py:234
  26.0 1.6 %collective-permute-start.2 = (f32[4,128,128]{2,1,0:T(8,128)S(1)}, f32[4,128,128]{2,1,0:T(8,128)S(1)}, u32[]{:S(2)}, u32[]{:S(2)}) collective-permute-start(f32[4,128,128]{2,1,0:T(8,128)S(1)} %pad_maximum_fusion.1), channel_id=1, source_target_pairs={{0,2},{1,3},{2,0},{3,1},{4,6},{5,7},{6,4},{7,5},{8,10},{9,11},{10,... | collective-permute-start | bytes 786440 | tf_op jit(solution)/shard_map/cond/branch_1_fun/ppermute | solution.py:234
  27.7 5.1 %collective-permute-done = f32[4,128,128]{2,1,0:T(8,128)S(1)} collective-permute-done((f32[4,128,128]{2,1,0:T(8,128)S(1)}, f32[4,128,128]{2,1,0:T(8,128)S(1)}, u32[]{:S(2)}, u32[]{:S(2)}) %collective-permute-start) | collective-permute-done | bytes 262176 | tf_op jit(solution)/shard_map/cond/branch_1_fun/ppermute | solution.py:234
  32.8 1.3 %collective-permute-done.2 = f32[4,128,128]{2,1,0:T(8,128)S(1)} collective-permute-done((f32[4,128,128]{2,1,0:T(8,128)S(1)}, f32[4,128,128]{2,1,0:T(8,128)S(1)}, u32[]{:S(2)}, u32[]{:S(2)}) %collective-permute-start.2) | collective-permute-done | bytes 262176 | tf_op jit(solution)/shard_map/cond/branch_1_fun/ppermute | solution.py:234
  34.2 1.6 %collective-permute-start.1 = (f32[2,128,128]{2,1,0:T(8,128)S(1)}, f32[2,128,128]{2,1,0:T(8,128)S(1)}, u32[]{:S(2)}, u32[]{:S(2)}) collective-permute-start(f32[2,128,128]{2,1,0:T(8,128)S(1)} %pad_maximum_fusion.2), channel_id=1, source_target_pairs={{0,2},{1,3},{2,0},{3,1},{4,6},{5,7},{6,4},{7,5},{8,10},{9,11},{10,... | collective-permute-start | bytes 393224 | tf_op jit(solution)/shard_map/cond/branch_1_fun/ppermute | solution.py:234
  35.8 1.5 %collective-permute-start.3 = (f32[2,128,128]{2,1,0:T(8,128)S(1)}, f32[2,128,128]{2,1,0:T(8,128)S(1)}, u32[]{:S(2)}, u32[]{:S(2)}) collective-permute-start(f32[2,128,128]{2,1,0:T(8,128)S(1)} %pad_maximum_fusion.3), channel_id=1, source_target_pairs={{0,1},{1,0},{2,3},{3,2},{4,5},{5,4},{6,7},{7,6},{8,9},{9,8},{10,11... | collective-permute-start | bytes 393224 | tf_op jit(solution)/shard_map/cond/branch_1_fun/ppermute | solution.py:234
  37.3 1.9 %collective-permute-done.1 = f32[2,128,128]{2,1,0:T(8,128)S(1)} collective-permute-done((f32[2,128,128]{2,1,0:T(8,128)S(1)}, f32[2,128,128]{2,1,0:T(8,128)S(1)}, u32[]{:S(2)}, u32[]{:S(2)}) %collective-permute-start.1) | collective-permute-done | bytes 131104 | tf_op jit(solution)/shard_map/cond/branch_1_fun/ppermute | solution.py:234
  39.2 1.6 %collective-permute-done.3 = f32[2,128,128]{2,1,0:T(8,128)S(1)} collective-permute-done((f32[2,128,128]{2,1,0:T(8,128)S(1)}, f32[2,128,128]{2,1,0:T(8,128)S(1)}, u32[]{:S(2)}, u32[]{:S(2)}) %collective-permute-start.3) | collective-permute-done | bytes 131104 | tf_op jit(solution)/shard_map/cond/branch_1_fun/ppermute | solution.py:234
  40.9 4.4 %collective-permute-start.4 = (f32[2,128,128]{2,1,0:T(8,128)S(1)}, f32[2,128,128]{2,1,0:T(8,128)S(1)}, u32[]{:S(2)}, u32[]{:S(2)}) collective-permute-start(f32[2,128,128]{2,1,0:T(8,128)S(1)} %pad_maximum_fusion.4), channel_id=1, source_target_pairs={{0,4},{1,5},{2,6},{3,7},{4,0},{5,1},{6,2},{7,3},{8,12},{9,13},{10,... | collective-permute-start | bytes 393224 | tf_op jit(solution)/shard_map/cond/branch_1_fun/ppermute | solution.py:234
  45.3 4.2 %collective-permute-done.4 = f32[2,128,128]{2,1,0:T(8,128)S(1)} collective-permute-done((f32[2,128,128]{2,1,0:T(8,128)S(1)}, f32[2,128,128]{2,1,0:T(8,128)S(1)}, u32[]{:S(2)}, u32[]{:S(2)}) %collective-permute-start.4) | collective-permute-done | bytes 131104 | tf_op jit(solution)/shard_map/cond/branch_1_fun/ppermute | solution.py:234
  49.5 0.0 copy-start
  49.6 0.0 copy-start.1
  49.6 0.0 collective-permute-done.6
  49.6 1.4 %add.71.refs_0_ = f32[16,128,128]{2,1,0:T(8,128)S(1)} add(f32[16,128,128]{2,1,0:T(8,128)S(1)} %get-tuple-element.60, f32[16,128,128]{2,1,0:T(8,128)} %collective-permute-done.6) | non-fusion elementwise | flops 262144 | bytes 3145728 | tf_op jit(solution)/shard_map/add | solution.py:290
  51.0 0.0 collective-permute-done.7
  51.0 1.2 %sum_parts.1 = f32[16,128,128]{2,1,0:T(8,128)} custom-call(f32[16,128,128]{2,1,0:T(8,128)S(1)} %add.71.refs_0_, f32[16,128,128]{2,1,0:T(8,128)S(1)} %bitcast.19), custom_call_target="tpu_custom_call" | custom-call | tf_op jit(solution)/shard_map/sum_parts/pallas_call | solution.py:222
  52.2 0.0 copy-done
  52.2 0.0 copy-done.1
  (11 shorter events, 0.2 us)
Async XLA Ops:
  15.7 3.7 %collective-permute-start.5 = (f32[1,16,128,128]{3,2,1,0:T(8,128)S(1)}, f32[1,16,128,128]{3,2,1,0:T(8,128)S(1)}, u32[]{:S(2)}, u32[]{:S(2)}) collective-permute-start(f32[1,16,128,128]{3,2,1,0:T(8,128)S(1)} %slice.79), channel_id=1, source_target_pairs={{0,8},{8,0},{16,24},{24,16},{1,9},{9,1},{17,25},{25,17},{2,10},{10... | collective-permute-start | bytes 3145736 | tf_op jit(solution)/shard_map/ppermute | solution.py:234
  21.0 28.6 %collective-permute-start.6 = (f32[16,128,128]{2,1,0:T(8,128)}, f32[16,128,128]{2,1,0:T(8,128)}, u32[]{:S(2)}, u32[]{:S(2)}) collective-permute-start(f32[16,128,128]{2,1,0:T(8,128)} %get-tuple-element.61), channel_id=1, source_target_pairs={{0,8},{8,0},{16,24},{24,16},{1,9},{9,1},{17,25},{25,17},{2,10},{10... | collective-permute-start | bytes 3145736 | tf_op jit(solution)/shard_map/ppermute | solution.py:234
  21.4 29.6 %collective-permute-start.7 = (f32[1,16,128,128]{3,2,1,0:T(8,128)}, f32[1,16,128,128]{3,2,1,0:T(8,128)S(1)}, u32[]{:S(2)}, u32[]{:S(2)}) collective-permute-start(f32[1,16,128,128]{3,2,1,0:T(8,128)} %bitcast.11), channel_id=1, source_target_pairs={{0,16},{8,24},{16,0},{24,8},{1,17},{9,25},{17,1},{25,9},{2,18},{10... | collective-permute-start | bytes 3145736 | tf_op jit(solution)/shard_map/ppermute | solution.py:234
  24.4 8.4 %collective-permute-start = (f32[4,128,128]{2,1,0:T(8,128)S(1)}, f32[4,128,128]{2,1,0:T(8,128)S(1)}, u32[]{:S(2)}, u32[]{:S(2)}) collective-permute-start(f32[4,128,128]{2,1,0:T(8,128)S(1)} %pad_maximum_fusion), channel_id=1, source_target_pairs={{0,1},{1,0},{2,3},{3,2},{4,5},{5,4},{6,7},{7,6},{8,9},{9,8},{10,11... | collective-permute-start | bytes 786440 | tf_op jit(solution)/shard_map/cond/branch_1_fun/ppermute | solution.py:234
  26.0 8.1 %collective-permute-start.2 = (f32[4,128,128]{2,1,0:T(8,128)S(1)}, f32[4,128,128]{2,1,0:T(8,128)S(1)}, u32[]{:S(2)}, u32[]{:S(2)}) collective-permute-start(f32[4,128,128]{2,1,0:T(8,128)S(1)} %pad_maximum_fusion.1), channel_id=1, source_target_pairs={{0,2},{1,3},{2,0},{3,1},{4,6},{5,7},{6,4},{7,5},{8,10},{9,11},{10,... | collective-permute-start | bytes 786440 | tf_op jit(solution)/shard_map/cond/branch_1_fun/ppermute | solution.py:234
  34.2 5.0 %collective-permute-start.1 = (f32[2,128,128]{2,1,0:T(8,128)S(1)}, f32[2,128,128]{2,1,0:T(8,128)S(1)}, u32[]{:S(2)}, u32[]{:S(2)}) collective-permute-start(f32[2,128,128]{2,1,0:T(8,128)S(1)} %pad_maximum_fusion.2), channel_id=1, source_target_pairs={{0,2},{1,3},{2,0},{3,1},{4,6},{5,7},{6,4},{7,5},{8,10},{9,11},{10,... | collective-permute-start | bytes 393224 | tf_op jit(solution)/shard_map/cond/branch_1_fun/ppermute | solution.py:234
  35.8 5.0 %collective-permute-start.3 = (f32[2,128,128]{2,1,0:T(8,128)S(1)}, f32[2,128,128]{2,1,0:T(8,128)S(1)}, u32[]{:S(2)}, u32[]{:S(2)}) collective-permute-start(f32[2,128,128]{2,1,0:T(8,128)S(1)} %pad_maximum_fusion.3), channel_id=1, source_target_pairs={{0,1},{1,0},{2,3},{3,2},{4,5},{5,4},{6,7},{7,6},{8,9},{9,8},{10,11... | collective-permute-start | bytes 393224 | tf_op jit(solution)/shard_map/cond/branch_1_fun/ppermute | solution.py:234
  40.9 8.6 %collective-permute-start.4 = (f32[2,128,128]{2,1,0:T(8,128)S(1)}, f32[2,128,128]{2,1,0:T(8,128)S(1)}, u32[]{:S(2)}, u32[]{:S(2)}) collective-permute-start(f32[2,128,128]{2,1,0:T(8,128)S(1)} %pad_maximum_fusion.4), channel_id=1, source_target_pairs={{0,4},{1,5},{2,6},{3,7},{4,0},{5,1},{6,2},{7,3},{8,12},{9,13},{10,... | collective-permute-start | bytes 393224 | tf_op jit(solution)/shard_map/cond/branch_1_fun/ppermute | solution.py:234
  49.5 2.7 %copy-start = (f32[128,128]{1,0:T(8,128)}, f32[128,128]{1,0:T(8,128)S(1)}, u32[]{:S(2)}) copy-start(f32[128,128]{1,0:T(8,128)S(1)} %get-tuple-element.55) | copy-start | bytes 196612
  49.6 2.7 %copy-start.1 = (f32[128,128]{1,0:T(8,128)}, f32[128,128]{1,0:T(8,128)S(1)}, u32[]{:S(2)}) copy-start(f32[128,128]{1,0:T(8,128)S(1)} %get-tuple-element.56) | copy-start | bytes 196612

commit v5 on v4

--- a/solution.py
+++ b/solution.py
@@ -280,17 +280,20 @@
     far = [j for j in range(2, ctx_size, 2)]
     got = swap(jnp.stack([dq[j | CORE] for j in far]), "ctx", ctx_size, CORE)
     parts = {j: dq[j] + got[n] for n, j in enumerate(far)}
-    own, near, dk, dv, parts = lax.optimization_barrier((dq[0], dq[CORE], dk, dv, parts))
+    near, dk, dv, parts = lax.optimization_barrier((dq[CORE], dk, dv, parts))
     arrived = []
     for bit in bits_of(ctx_size)[1:]:
         sent = [j for j in sorted(parts) if j & bit]
         got = dict(zip(sent, swap(jnp.stack([parts[j] for j in sent]), "ctx", ctx_size, bit)))
         arrived.append(got.pop(bit))
         parts = {j: parts[j] + got[j | bit] for j in parts if not j & bit}
-    own = lax.optimization_barrier(own + swap(near, "ctx", ctx_size, CORE))
+    near = swap(near, "ctx", ctx_size, CORE)
     by_dest = lambda a: {j: a[j] for j in range(pb_size)}
-    sums = partial(sum_two_ways, axis="pb", size=pb_size)
-    key_grad, value_grad = in_one_piece(sums, by_dest(dk), by_dest(dv))
+
+    def sums(dk, dv, own, near):
+        return *sum_two_ways(by_dest(dk), by_dest(dv), "pb", pb_size), own[0] + near
+
+    key_grad, value_grad, own = in_one_piece(sums, dk, dv, dq, near)
     query_grad = sum_in_hbm([own] + arrived)
     return query_grad.reshape(questions, tokens // ctx_size, heads, width), key_grad, value_grad
 

time: 52.9 us -> 52.4 us (level); the launches traced: 52.2 us -> 53.1 us
  Pallas kernels: 16.2 us -> 20 us
  starting transfers between devices: 15.4 us -> 11.7 us
    pallas_call x1, Pallas kernels: 14.9 us -> 18.7 us  [backward(): pl.pallas_call(partial(backward_kernel, width ** (-0.5)), in_specs=[pl.Bl...]
    ppermute x8, starting transfers between devices: 15.4 us -> 11.7 us  [swap(): return lax.ppermute(array, axis, [(i, i ^ bit) for i in range(size)])]
  transfers between devices with their start and end apart: 8 -> 8, of which waited for: 6 -> 7; matrix products, arithmetic and copies ran while one was open for 3% -> 3% of each run, Pallas kernels for 0% -> 0%
where the time goes in v5:
time: 52.4 us; the launch traced here: 53.1 us
  Pallas kernels  20 us (38%)
  waiting for transfers between devices  17 us (32%)
  starting transfers between devices  11.7 us (22%)
  other arithmetic  3.4 us (6%)
  between operations  0.71 us (1%)
    pallas_call x1, Pallas kernels, backward(): pl.pallas_call(partial(backward_kernel, width ** (-0.5)), in_specs=[pl.Bl...  18.7 us
    ppermute x8, waiting for transfers between devices, swap(): return lax.ppermute(array, axis, [(i, i ^ bit) for i in range(size)])  17 us
    ppermute x8, starting transfers between devices, swap(): return lax.ppermute(array, axis, [(i, i ^ bit) for i in range(size)])  11.7 us
    add x1, other arithmetic, sums(): own[0] + near  1.67 us
    add x1, other arithmetic, local(): parts = {j: dq[j] + got[n] for n, j in enumerate(far)}  1.58 us
    pallas_call x1, Pallas kernels, sum_in_hbm(): pl.pallas_call(partial(sum_kernel, cuts), in_specs=[pl.BlockSpec(memory_s...  1.33 us
  transfers between devices with their start and end apart: 8, of which 7 were waited for; matrix products, arithmetic and copies ran while one was open for 3% of the time, Pallas kernels for 0%

profile of v5, /device:TPU:0, one launch (start us, length us, event | category | flops | bytes accessed | tf_op | source)
XLA Modules:
  0.0 53.1 jit_solution(10507783533853267194)
XLA Ops:
  0.6 18.7 %attention_backward.1 = (f32[4,16,128,128]{3,2,1,0:T(8,128)S(1)}, f32[8,128,128]{2,1,0:T(8,128)S(1)}, f32[8,128,128]{2,1,0:T(8,128)S(1)}) custom-call(s32[16,24]{1,0:T(8,128)} %lists_hbm.1, f32[16,8,64]{2,1,0:T(8,128)} %bitcast.26, bf16[16,512,128]{2,1,0:T(8,128)(2,1)} %bitcast.21, bf16[16,512,128]{2,1,0:T(8,128)(2,1)} %bitcast.22, ...), custom_call_target="tpu_custom_call" | custom-call | flops 10737418240 | bytes 12582912 | tf_op jit(solution)/shard_map/attention_backward/pallas_call | solution.py:174
  19.3 0.0 copy-start
  19.3 0.1 slice.60
  19.4 0.1 collective-permute-start.5
  19.5 2.6 %collective-permute-done.5 = f32[1,16,128,128]{3,2,1,0:T(8,128)S(1)} collective-permute-done((f32[1,16,128,128]{3,2,1,0:T(8,128)S(1)}, f32[1,16,128,128]{3,2,1,0:T(8,128)S(1)}, u32[]{:S(2)}, u32[]{:S(2)}) %collective-permute-start.5) | collective-permute-done | bytes 1048608 | tf_op jit(solution)/shard_map/ppermute | solution.py:234
  22.2 0.0 copy-done
  22.2 1.6 %add_bitcast_fusion = (f32[16,128,128]{2,1,0:T(8,128)}, f32[16,128,128]{2,1,0:T(8,128)}) fusion(f32[1,16,128,128]{3,2,1,0:T(8,128)S(1)} %collective-permute-done.5, f32[4,16,128,128]{3,2,1,0:T(8,128)S(1)} %get-tuple-element.25), kind=kLoop, calls=%fused_computation.22 | loop fusion | flops 262144 | bytes 5242880 | tf_op jit(solution)/shard_map/add | solution.py:282
  23.7 0.1 collective-permute-start.6
  23.9 0.9 %collective-permute-start.7 = (f32[1,16,128,128]{3,2,1,0:T(8,128)}, f32[1,16,128,128]{3,2,1,0:T(8,128)S(1)}, u32[]{:S(2)}, u32[]{:S(2)}) collective-permute-start(f32[1,16,128,128]{3,2,1,0:T(8,128)} %bitcast.11), channel_id=1, source_target_pairs={{0,16},{8,24},{16,0},{24,8},{1,17},{9,25},{17,1},{25,9},{2,18},{10... | collective-permute-start | bytes 3145736 | tf_op jit(solution)/shard_map/ppermute | solution.py:234
  24.8 1.8 %collective-permute-done.6 = f32[16,128,128]{2,1,0:T(8,128)S(1)} collective-permute-done((f32[16,128,128]{2,1,0:T(8,128)}, f32[16,128,128]{2,1,0:T(8,128)S(1)}, u32[]{:S(2)}, u32[]{:S(2)}) %collective-permute-start.6) | collective-permute-done | bytes 1048608 | tf_op jit(solution)/shard_map/ppermute | solution.py:234
  26.6 25.1 %conditional.1 = (f32[128,128]{1,0:T(8,128)S(1)}, f32[128,128]{1,0:T(8,128)S(1)}, f32[16,128,128]{2,1,0:T(8,128)S(1)}) conditional(s32[]{:T(128)} %convert_element_type.3, () %tuple.17, (f32[8,128,128]{2,1,0:T(8,128)S(1)}, f32[8,128,128]{2,1,0:T(8,128)S(1)}, f32[4,16,128,128]{3,2,1,0:T(8,128)}, f32[16,128,128]{2,1,0:T(8,128)S(1)}) %tuple.33), branch_computations={%region_0.0_spmd, %region_1.0_spmd} | conditional | flops 851968 | bytes 15859964 | solution.py:262
  26.6 0.0 copy-start.1
  26.7 1.4 %collective-permute-start.2 = (f32[4,128,128]{2,1,0:T(8,128)S(1)}, f32[4,128,128]{2,1,0:T(8,128)S(1)}, u32[]{:S(2)}, u32[]{:S(2)}) collective-permute-start(f32[4,128,128]{2,1,0:T(8,128)S(1)} %pad_maximum_fusion.1), channel_id=1, source_target_pairs={{0,2},{1,3},{2,0},{3,1},{4,6},{5,7},{6,4},{7,5},{8,10},{9,11},{10,... | collective-permute-start | bytes 786440 | tf_op jit(solution)/shard_map/cond/branch_1_fun/ppermute | solution.py:234
  28.1 2.8 %collective-permute-start = (f32[4,128,128]{2,1,0:T(8,128)S(1)}, f32[4,128,128]{2,1,0:T(8,128)S(1)}, u32[]{:S(2)}, u32[]{:S(2)}) collective-permute-start(f32[4,128,128]{2,1,0:T(8,128)S(1)} %pad_maximum_fusion), channel_id=1, source_target_pairs={{0,1},{1,0},{2,3},{3,2},{4,5},{5,4},{6,7},{7,6},{8,9},{9,8},{10,11... | collective-permute-start | bytes 786440 | tf_op jit(solution)/shard_map/cond/branch_1_fun/ppermute | solution.py:234
  30.8 4.2 %collective-permute-done.2 = f32[4,128,128]{2,1,0:T(8,128)S(1)} collective-permute-done((f32[4,128,128]{2,1,0:T(8,128)S(1)}, f32[4,128,128]{2,1,0:T(8,128)S(1)}, u32[]{:S(2)}, u32[]{:S(2)}) %collective-permute-start.2) | collective-permute-done | bytes 262176 | tf_op jit(solution)/shard_map/cond/branch_1_fun/ppermute | solution.py:234
  35.1 2.3 %collective-permute-done = f32[4,128,128]{2,1,0:T(8,128)S(1)} collective-permute-done((f32[4,128,128]{2,1,0:T(8,128)S(1)}, f32[4,128,128]{2,1,0:T(8,128)S(1)}, u32[]{:S(2)}, u32[]{:S(2)}) %collective-permute-start) | collective-permute-done | bytes 262176 | tf_op jit(solution)/shard_map/cond/branch_1_fun/ppermute | solution.py:234
  37.4 0.4 collective-permute-start.1
  37.8 1.8 %collective-permute-start.3 = (f32[2,128,128]{2,1,0:T(8,128)S(1)}, f32[2,128,128]{2,1,0:T(8,128)S(1)}, u32[]{:S(2)}, u32[]{:S(2)}) collective-permute-start(f32[2,128,128]{2,1,0:T(8,128)S(1)} %pad_maximum_fusion.3), channel_id=1, source_target_pairs={{0,1},{1,0},{2,3},{3,2},{4,5},{5,4},{6,7},{7,6},{8,9},{9,8},{10,11... | collective-permute-start | bytes 393224 | tf_op jit(solution)/shard_map/cond/branch_1_fun/ppermute | solution.py:234
  39.6 2.8 %collective-permute-done.1 = f32[2,128,128]{2,1,0:T(8,128)S(1)} collective-permute-done((f32[2,128,128]{2,1,0:T(8,128)S(1)}, f32[2,128,128]{2,1,0:T(8,128)S(1)}, u32[]{:S(2)}, u32[]{:S(2)}) %collective-permute-start.1) | collective-permute-done | bytes 131104 | tf_op jit(solution)/shard_map/cond/branch_1_fun/ppermute | solution.py:234
  42.5 0.4 collective-permute-done.3
  42.9 4.2 %collective-permute-start.4 = (f32[2,128,128]{2,1,0:T(8,128)S(1)}, f32[2,128,128]{2,1,0:T(8,128)S(1)}, u32[]{:S(2)}, u32[]{:S(2)}) collective-permute-start(f32[2,128,128]{2,1,0:T(8,128)S(1)} %pad_maximum_fusion.4), channel_id=1, source_target_pairs={{0,4},{1,5},{2,6},{3,7},{4,0},{5,1},{6,2},{7,3},{8,12},{9,13},{10,... | collective-permute-start | bytes 393224 | tf_op jit(solution)/shard_map/cond/branch_1_fun/ppermute | solution.py:234
  47.1 0.0 copy-done.1
  47.1 1.7 %bitcast_add_fusion = f32[16,128,128]{2,1,0:T(8,128)S(1)} fusion(f32[16,128,128]{2,1,0:T(8,128)} %copy-done.1, f32[4,16,128,128]{3,2,1,0:T(8,128)} %get-tuple-element.10), kind=kLoop, calls=%fused_computation | loop fusion | flops 262144 | bytes 3145728 | tf_op jit(solution)/shard_map/cond/branch_1_fun/add | solution.py:294
  48.8 2.9 %collective-permute-done.4 = f32[2,128,128]{2,1,0:T(8,128)S(1)} collective-permute-done((f32[2,128,128]{2,1,0:T(8,128)S(1)}, f32[2,128,128]{2,1,0:T(8,128)S(1)}, u32[]{:S(2)}, u32[]{:S(2)}) %collective-permute-start.4) | collective-permute-done | bytes 131104 | tf_op jit(solution)/shard_map/cond/branch_1_fun/ppermute | solution.py:234
  51.7 0.0 copy-start.2
  51.7 0.0 copy-start.3
  51.7 0.0 collective-permute-done.7
  51.7 1.3 %sum_parts.1 = f32[16,128,128]{2,1,0:T(8,128)} custom-call(f32[16,128,128]{2,1,0:T(8,128)S(1)} %get-tuple-element.31.refs_0_, f32[16,128,128]{2,1,0:T(8,128)S(1)} %bitcast.19), custom_call_target="tpu_custom_call" | custom-call | tf_op jit(solution)/shard_map/sum_parts/pallas_call | solution.py:222
  53.1 0.0 copy-done.2
  53.1 0.0 copy-done.3
  (11 shorter events, 0.2 us)
Async XLA Ops:
  19.3 2.8 %copy-start = (f32[4,16,128,128]{3,2,1,0:T(8,128)}, f32[4,16,128,128]{3,2,1,0:T(8,128)S(1)}, u32[]{:S(2)}) copy-start(f32[4,16,128,128]{3,2,1,0:T(8,128)S(1)} %get-tuple-element.25) | copy-start | bytes 12582916
  19.4 2.7 %collective-permute-start.5 = (f32[1,16,128,128]{3,2,1,0:T(8,128)S(1)}, f32[1,16,128,128]{3,2,1,0:T(8,128)S(1)}, u32[]{:S(2)}, u32[]{:S(2)}) collective-permute-start(f32[1,16,128,128]{3,2,1,0:T(8,128)S(1)} %slice.60), channel_id=1, source_target_pairs={{0,8},{8,0},{16,24},{24,16},{1,9},{9,1},{17,25},{25,17},{2,10},{10... | collective-permute-start | bytes 3145736 | tf_op jit(solution)/shard_map/ppermute | solution.py:234
  23.7 2.9 %collective-permute-start.6 = (f32[16,128,128]{2,1,0:T(8,128)}, f32[16,128,128]{2,1,0:T(8,128)S(1)}, u32[]{:S(2)}, u32[]{:S(2)}) collective-permute-start(f32[16,128,128]{2,1,0:T(8,128)} %get-tuple-element.30), channel_id=1, source_target_pairs={{0,8},{8,0},{16,24},{24,16},{1,9},{9,1},{17,25},{25,17},{2,10},{10... | collective-permute-start | bytes 3145736 | tf_op jit(solution)/shard_map/ppermute | solution.py:234
  23.9 27.8 %collective-permute-start.7 = (f32[1,16,128,128]{3,2,1,0:T(8,128)}, f32[1,16,128,128]{3,2,1,0:T(8,128)S(1)}, u32[]{:S(2)}, u32[]{:S(2)}) collective-permute-start(f32[1,16,128,128]{3,2,1,0:T(8,128)} %bitcast.11), channel_id=1, source_target_pairs={{0,16},{8,24},{16,0},{24,8},{1,17},{9,25},{17,1},{25,9},{2,18},{10... | collective-permute-start | bytes 3145736 | tf_op jit(solution)/shard_map/ppermute | solution.py:234
  26.6 20.5 %copy-start.1 = (f32[16,128,128]{2,1,0:T(8,128)}, f32[16,128,128]{2,1,0:T(8,128)S(1)}, u32[]{:S(2)}) copy-start(f32[16,128,128]{2,1,0:T(8,128)S(1)} %get-tuple-element.11) | copy-start | bytes 3145732 | tf_op jit(solution)/shard_map/cond
  26.7 8.4 %collective-permute-start.2 = (f32[4,128,128]{2,1,0:T(8,128)S(1)}, f32[4,128,128]{2,1,0:T(8,128)S(1)}, u32[]{:S(2)}, u32[]{:S(2)}) collective-permute-start(f32[4,128,128]{2,1,0:T(8,128)S(1)} %pad_maximum_fusion.1), channel_id=1, source_target_pairs={{0,2},{1,3},{2,0},{3,1},{4,6},{5,7},{6,4},{7,5},{8,10},{9,11},{10,... | collective-permute-start | bytes 786440 | tf_op jit(solution)/shard_map/cond/branch_1_fun/ppermute | solution.py:234
  28.1 9.3 %collective-permute-start = (f32[4,128,128]{2,1,0:T(8,128)S(1)}, f32[4,128,128]{2,1,0:T(8,128)S(1)}, u32[]{:S(2)}, u32[]{:S(2)}) collective-permute-start(f32[4,128,128]{2,1,0:T(8,128)S(1)} %pad_maximum_fusion), channel_id=1, source_target_pairs={{0,1},{1,0},{2,3},{3,2},{4,5},{5,4},{6,7},{7,6},{8,9},{9,8},{10,11... | collective-permute-start | bytes 786440 | tf_op jit(solution)/shard_map/cond/branch_1_fun/ppermute | solution.py:234
  37.4 5.0 %collective-permute-start.1 = (f32[2,128,128]{2,1,0:T(8,128)S(1)}, f32[2,128,128]{2,1,0:T(8,128)S(1)}, u32[]{:S(2)}, u32[]{:S(2)}) collective-permute-start(f32[2,128,128]{2,1,0:T(8,128)S(1)} %pad_maximum_fusion.2), channel_id=1, source_target_pairs={{0,2},{1,3},{2,0},{3,1},{4,6},{5,7},{6,4},{7,5},{8,10},{9,11},{10,... | collective-permute-start | bytes 393224 | tf_op jit(solution)/shard_map/cond/branch_1_fun/ppermute | solution.py:234
  37.8 5.0 %collective-permute-start.3 = (f32[2,128,128]{2,1,0:T(8,128)S(1)}, f32[2,128,128]{2,1,0:T(8,128)S(1)}, u32[]{:S(2)}, u32[]{:S(2)}) collective-permute-start(f32[2,128,128]{2,1,0:T(8,128)S(1)} %pad_maximum_fusion.3), channel_id=1, source_target_pairs={{0,1},{1,0},{2,3},{3,2},{4,5},{5,4},{6,7},{7,6},{8,9},{9,8},{10,11... | collective-permute-start | bytes 393224 | tf_op jit(solution)/shard_map/cond/branch_1_fun/ppermute | solution.py:234
  42.9 8.8 %collective-permute-start.4 = (f32[2,128,128]{2,1,0:T(8,128)S(1)}, f32[2,128,128]{2,1,0:T(8,128)S(1)}, u32[]{:S(2)}, u32[]{:S(2)}) collective-permute-start(f32[2,128,128]{2,1,0:T(8,128)S(1)} %pad_maximum_fusion.4), channel_id=1, source_target_pairs={{0,4},{1,5},{2,6},{3,7},{4,0},{5,1},{6,2},{7,3},{8,12},{9,13},{10,... | collective-permute-start | bytes 393224 | tf_op jit(solution)/shard_map/cond/branch_1_fun/ppermute | solution.py:234
  51.7 1.4 %copy-start.2 = (f32[128,128]{1,0:T(8,128)}, f32[128,128]{1,0:T(8,128)S(1)}, u32[]{:S(2)}) copy-start(f32[128,128]{1,0:T(8,128)S(1)} %get-tuple-element.24) | copy-start | bytes 196612
  51.7 1.4 %copy-start.3 = (f32[128,128]{1,0:T(8,128)}, f32[128,128]{1,0:T(8,128)S(1)}, u32[]{:S(2)}) copy-start(f32[128,128]{1,0:T(8,128)S(1)} %get-tuple-element.23) | copy-start | bytes 196612
